TPU v7x, 128 devices: a whole 4x4x4 slice. The times are simulated.
128 devices in a mesh: freq: 32 (over y, x, core), tm: 4 (over z).
Axes of the slice: x: 4, y: 4, z: 4, core: 2. Of those that a mesh axis runs over, the one named last changes fastest.
Arguments:
- voltages: bfloat16 [2, 1024, 128, 1024], P(None, 'tm', 'freq'), may hold values from -6 to 6
- gains: float32 [2, 128, 1024], P(None, 'freq'), may hold values from -5 to 5
- window: float32 [64], replicated, may hold values from 0.2 to 1
Outputs:
- intensity: float32 [1024, 16, 2048], P('freq', 'tm')
All inputs are finite; a program needn't handle non-finite values.
Results may differ from a plain program's by a relative error of at most 0.0065.
Values may be sent and summed in bfloat16 or wider, within the bound.
No kernel may reach another device: no remote copies, remote signals or barrier semaphores. Data moves between devices by JAX's collectives and lax.ppermute only.
A program may use at most 128 MiB of HBM per device.

v0:
```python
import math

import jax
import jax.numpy as jnp
import numpy as np
from jax import lax
from jax.experimental import pallas as pl
from jax.experimental.pallas import tpu as pltpu
from jax.sharding import PartitionSpec as P

EW = 4
NS = 256
FEEDS = EW * NS
FINE = 16
TAPS = 4
INTEG = 4
CHAN = 4
SPAN = INTEG * FINE
PAST = (TAPS - 1) * FINE
GROUP = 32
HALF = 16
TIMES = 4

F32 = jnp.float32
BF16 = jnp.bfloat16


def fine_tables():
    f = np.arange(FINE)[:, None]
    n = np.arange(2 * SPAN)[None, :] % FINE
    angle = (f * n % FINE) * (2.0 * math.pi / FINE)
    scale = 1.0 / math.sqrt(FINE * TAPS)
    return np.stack([np.cos(angle), np.sin(angle)]).astype(np.float32) * np.float32(scale)


def beam_table():
    q = np.arange(NS)[:, None]
    lane = np.arange(NS)[None, :]
    k = (lane % 128) // HALF * GROUP + lane // 128 * HALF + lane % HALF
    angle = (q * k % NS).astype(np.float32) * np.float32(2.0 * math.pi / NS)
    cos = np.cos(angle).astype(jnp.bfloat16).astype(np.float32)
    sin = np.sin(angle).astype(jnp.bfloat16).astype(np.float32)
    scale = 1.0 / math.sqrt(NS) / math.sqrt(EW) / math.sqrt(INTEG)
    table = np.block([[cos, -sin], [sin, cos]]) * np.float32(scale)
    return table.astype(jnp.bfloat16)


def fill_bank(window_ref, fine_ref, bank_ref):
    taps = jnp.concatenate([window_ref[...], jnp.zeros((1, 64), F32)], axis=1)
    lane = lax.broadcasted_iota(jnp.int32, (1, 2 * SPAN), 1)
    line = jnp.zeros((1, 2 * SPAN), F32)
    for m in range(TAPS):
        moved = pltpu.roll(taps, (64 - 32 * m) % 128, 1)
        line = jnp.where(lane // FINE == TAPS - m, moved, line)
    cos, sin = fine_ref[0], fine_ref[1]
    for j in range(INTEG):
        row = line if j == 0 else pltpu.roll(line, FINE * j, 1)
        re, im = (cos * row).astype(BF16), (sin * row).astype(BF16)
        bank_ref[FINE * j : FINE * (j + 1), :128] = re
        bank_ref[FINE * j : FINE * (j + 1), 128:] = im
        bank_ref[64 + FINE * j : 64 + FINE * (j + 1), :128] = -im
        bank_ref[64 + FINE * j : 64 + FINE * (j + 1), 128:] = re


def form_time(now, past_of, gains_ref, table_ref, bank_ref, left_ref, out_ref):
    for c in range(CHAN):
        data = jnp.concatenate(
            [past_of(0, c), now[0][c], past_of(1, c), now[1][c]], axis=0
        )
        spec = jnp.dot(bank_ref[...], data, preferred_element_type=F32)
        sr, si = spec[:SPAN], spec[SPAN:]
        gr, gi = gains_ref[0, c : c + 1], gains_ref[1, c : c + 1]
        cr = gr * sr - gi * si
        ci = gr * si + gi * sr
        r0, r1, r2, r3 = (cr[:, NS * e : NS * (e + 1)] for e in range(EW))
        i0, i1, i2, i3 = (ci[:, NS * e : NS * (e + 1)] for e in range(EW))
        rs, rd, it, iu = r0 + r2, r0 - r2, i0 + i2, i0 - i2
        rv, rw, iv, iw = r1 + r3, r1 - r3, i1 + i3, i1 - i3
        beams = ((rs + rv, it + iv), (rd + iw, iu - rw), (rs - rv, it - iv), (rd - iw, iu + rw))
        for g in range(EW):
            re, im = beams[g][0].astype(BF16), beams[g][1].astype(BF16)
            for j in range(INTEG):
                at = 256 * g + 64 * j + FINE * c
                left_ref[at : at + FINE, :NS] = re[FINE * j : FINE * (j + 1)]
                left_ref[at : at + FINE, NS:] = im[FINE * j : FINE * (j + 1)]
    for g in range(EW):
        beam = jnp.dot(
            left_ref[256 * g : 256 * (g + 1)], table_ref[...], preferred_element_type=F32
        )
        re, im = beam[:, :NS], beam[:, NS:]
        power = re * re + im * im
        power = power[:64] + power[64:128] + power[128:192] + power[192:]
        power = jnp.concatenate([power[:, :128], power[:, 128:]], axis=0)
        out_ref[8 * g : 8 * (g + 1)] = power.T.astype(BF16).reshape(8, HALF, 128)


def later_kernel(volt_ref, gains_ref, window_ref, fine_ref, table_ref, out_ref, bank_ref, kept_ref, left_ref):
    step = pl.program_id(0)

    @pl.when(step == 0)
    def _():
        fill_bank(window_ref, fine_ref, bank_ref)
        for part in range(2):
            kept_ref[part] = jnp.swapaxes(volt_ref[part], 0, 1)

    @pl.when(step > 0)
    def _():
        now = [jnp.swapaxes(volt_ref[part], 0, 1) for part in range(2)]
        form_time(now, lambda part, c: kept_ref[part, c], gains_ref, table_ref, bank_ref, left_ref, out_ref)
        for part in range(2):
            kept_ref[part] = now[part]


def first_kernel(volt_ref, halo_ref, gains_ref, window_ref, fine_ref, table_ref, rest_ref, out_ref, bank_ref, left_ref):
    fill_bank(window_ref, fine_ref, bank_ref)
    now = [jnp.swapaxes(volt_ref[part], 0, 1) for part in range(2)]
    past = [jnp.swapaxes(halo_ref[part], 0, 1) for part in range(2)]
    zeros = jnp.zeros((SPAN - PAST, FEEDS), BF16)
    form_time(
        now, lambda part, c: jnp.concatenate([zeros, past[part][c]], axis=0),
        gains_ref, table_ref, bank_ref, left_ref, out_ref,
    )


def join_kernel(got_ref, out_ref):
    lane = lax.broadcasted_iota(jnp.int32, (1, 128), 1)
    low = lane < 64
    for s in range(GROUP // 2):
        a = got_ref[2 * s].astype(F32)
        b = got_ref[2 * s + 1].astype(F32)
        first = jnp.where(low, a, pltpu.roll(b, 64, 1)).reshape(TIMES, HALF, 128)
        second = jnp.where(low, pltpu.roll(a, 64, 1), b).reshape(TIMES, HALF, 128)
        out_ref[:HALF, :, 128 * s : 128 * (s + 1)] = jnp.swapaxes(first, 0, 1)
        out_ref[HALF:, :, 128 * s : 128 * (s + 1)] = jnp.swapaxes(second, 0, 1)


PARAMS = pltpu.CompilerParams(vmem_limit_bytes=48 << 20)


def whole(*shape):
    return pl.BlockSpec(shape, lambda *_: (0,) * len(shape))


def body(voltages, gains, window):
    samples = voltages.shape[1]
    halo = voltages[:, samples - PAST :]
    count = lax.axis_size("tm")
    halo = lax.ppermute(halo, "tm", [(i, i + 1) for i in range(count - 1)])
    fine = jnp.asarray(fine_tables())
    table = jnp.asarray(beam_table())
    window = window.reshape(1, FINE * TAPS)
    shape = jax.ShapeDtypeStruct((GROUP, TIMES * HALF, 128), BF16)
    shared = [
        whole(2, CHAN, FEEDS), whole(1, FINE * TAPS), whole(2, FINE, 2 * SPAN), whole(2 * NS, 2 * NS)
    ]
    flops = 2 * (4 * 128 * 256 * 1024 + 1024 * 512 * 512)
    rest = pl.pallas_call(
        later_kernel,
        grid=(TIMES,),
        in_specs=[pl.BlockSpec((2, SPAN, CHAN, FEEDS), lambda t: (0, t, 0, 0))] + shared,
        out_specs=pl.BlockSpec((GROUP, HALF, 128), lambda t: (0, jnp.maximum(t, 1), 0)),
        out_shape=shape,
        scratch_shapes=[
            pltpu.VMEM((128, 256), BF16),
            pltpu.VMEM((2, CHAN, SPAN, FEEDS), BF16),
            pltpu.VMEM((1024, 512), BF16),
        ],
        compiler_params=PARAMS,
        cost_estimate=pl.CostEstimate(flops=3 * flops, bytes_accessed=5 << 20, transcendentals=0),
        name="later_times",
    )(voltages, gains, window, fine, table)
    power = pl.pallas_call(
        first_kernel,
        grid=(1,),
        in_specs=[
            pl.BlockSpec((2, SPAN, CHAN, FEEDS), lambda t: (0, 0, 0, 0)),
            whole(2, PAST, CHAN, FEEDS),
        ] + shared + [pl.BlockSpec(memory_space=pl.ANY)],
        out_specs=pl.BlockSpec((GROUP, HALF, 128), lambda t: (0, 0, 0)),
        out_shape=shape,
        scratch_shapes=[pltpu.VMEM((128, 256), BF16), pltpu.VMEM((1024, 512), BF16)],
        input_output_aliases={6: 0},
        compiler_params=PARAMS,
        cost_estimate=pl.CostEstimate(flops=flops, bytes_accessed=3 << 20, transcendentals=0),
        name="first_time",
    )(voltages, halo, gains, window, fine, table, rest)
    got = lax.all_to_all(power, "freq", split_axis=0, concat_axis=0, tiled=True)
    return pl.pallas_call(
        join_kernel,
        out_shape=jax.ShapeDtypeStruct((GROUP, TIMES, GROUP * CHAN * FINE), F32),
        compiler_params=PARAMS,
        name="join_channels",
    )(got)


def solution(mesh):
    placed = (P(None, "tm", "freq", None), P(None, "freq", None), P())
    return jax.shard_map(
        body, mesh=mesh, in_specs=placed, out_specs=P("freq", "tm", None), check_vma=False
    )
```

profile of v0, /device:TPU:1, one launch (start us, length us, event | category | flops | bytes accessed | tf_op | source)
XLA Modules:
  0.0 45.3 jit_solution(5962145356426125150)
XLA Ops:
  0.0 1.4 %slice.3 = bf16[2,48,4,1024]{3,2,1,0:T(4,128)(2,1)S(1)} slice(bf16[2,256,4,1024]{3,2,1,0:T(4,128)(2,1)} %volt_ref.3), slice={[0:2], [208:256], [0:4], [0:1024]} | slice | bytes 1572864 | tf_op jit(solution)/shard_map/slice | solution.py:146
  1.4 4.4 %collective-permute-start = (bf16[2,48,4,1024]{3,2,1,0:T(4,128)(2,1)S(1)}, bf16[2,48,4,1024]{3,2,1,0:T(4,128)(2,1)S(1)}, u32[]{:S(2)}, u32[]{:S(2)}) collective-permute-start(bf16[2,48,4,1024]{3,2,1,0:T(4,128)(2,1)S(1)} %slice.3), channel_id=1, source_target_pairs={{0,1},{1,2},{2,3},{4,5},{5,6},{6,7},{8,9},{9,10},{10,11},{12,13},{... | collective-permute-start | bytes 2359304 | tf_op jit(solution)/shard_map/ppermute | solution.py:148
  5.8 0.0 copy-start
  5.8 2.2 %copy-done = bf16[2,256,4,1024]{3,2,1,0:T(4,128)(2,1)S(1)} copy-done((bf16[2,256,4,1024]{3,2,1,0:T(4,128)(2,1)S(1)}, bf16[2,256,4,1024]{3,2,1,0:T(4,128)(2,1)}, u32[]{:S(2)}) %copy-start) | copy-done | bytes 4194328
  8.0 0.0 copy-start.1
  8.0 1.0 %copy-done.1 = bf16[512,512]{1,0:T(8,128)(2,1)S(1)} copy-done((bf16[512,512]{1,0:T(8,128)(2,1)S(1)}, bf16[512,512]{1,0:T(8,128)(2,1)}, u32[]{:S(2)}) %copy-start.1) | copy-done | bytes 524312
  9.1 0.0 copy-start.2
  9.1 0.8 %copy-done.2 = f32[2,4,1024]{2,1,0:T(4,128)S(1)} copy-done((f32[2,4,1024]{2,1,0:T(4,128)S(1)}, f32[2,4,1024]{2,1,0:T(4,128)}, u32[]{:S(2)}) %copy-start.2) | copy-done | bytes 32792
  9.8 0.0 copy-start.3
  9.8 0.7 %copy-done.3 = f32[2,16,128]{2,1,0:T(8,128)S(1)} copy-done((f32[2,16,128]{2,1,0:T(8,128)S(1)}, f32[2,16,128]{2,1,0:T(8,128)}, u32[]{:S(2)}) %copy-start.3) | copy-done | bytes 16408
  10.5 0.0 copy-start.4
  10.5 0.7 %copy-done.4 = f32[64]{0:T(128)S(1)} copy-done((f32[64]{0:T(128)S(1)}, f32[64]{0:T(128)}, u32[]{:S(2)}) %copy-start.4) | copy-done | bytes 280
  11.2 5.8 %later_times.1.rest_ref = bf16[32,64,128]{2,1,0:T(8,128)(2,1)S(1)} custom-call(bf16[2,256,4,1024]{3,2,1,0:T(4,128)(2,1)S(1)} %copy-done, f32[2,4,1024]{2,1,0:T(4,128)S(1)} %copy-done.2, f32[1,64]{1,0:T(1,128)S(1)} %bitcast.1, f32[2,16,128]{2,1,0:T(8,128)S(1)} %copy-done.3, bf16[512,512]{1,0:T(8,128)(2,1)S(1)} %copy-done.1), custom_call_target="tpu_custom_call" | custom-call | flops 2415919104 | bytes 5242880 | tf_op jit(solution)/shard_map/later_times/pallas_call | solution.py:157
  17.0 5.0 %collective-permute-done.halo_ref = bf16[2,48,4,1024]{3,2,1,0:T(4,128)(2,1)S(1)} collective-permute-done((bf16[2,48,4,1024]{3,2,1,0:T(4,128)(2,1)S(1)}, bf16[2,48,4,1024]{3,2,1,0:T(4,128)(2,1)S(1)}, u32[]{:S(2)}, u32[]{:S(2)}) %collective-permute-start) | collective-permute-done | bytes 786464 | tf_op jit(solution)/shard_map/ppermute | solution.py:148
  22.0 1.9 %first_time.1 = bf16[32,64,128]{2,1,0:T(8,128)(2,1)S(1)} custom-call(bf16[2,256,4,1024]{3,2,1,0:T(4,128)(2,1)S(1)} %copy-done, bf16[2,48,4,1024]{3,2,1,0:T(4,128)(2,1)S(1)} %collective-permute-done.halo_ref, f32[2,4,1024]{2,1,0:T(4,128)S(1)} %copy-done.2, f32[1,64]{1,0:T(1,128)S(1)} %bitcast.2, ...), custom_call_target="tpu_custom_call", output_to_operand_aliasing={{}: (6, {})} | custom-call | flops 805306368 | bytes 3145728 | tf_op jit(solution)/shard_map/first_time/pallas_call | solution.py:172
  23.9 20.0 %all_to_all.5.got_ref = bf16[32,64,128]{2,1,0:T(8,128)(2,1)S(1)} all-to-all(bf16[32,64,128]{2,1,0:T(8,128)(2,1)S(1)} %first_time.1), channel_id=1, replica_groups=mesh['freq'=32,'tm'=4] {'freq'}, dimensions={0} | all-to-all | bytes 1048576 | tf_op jit(solution)/shard_map/all_to_all | solution.py:187
  43.9 1.4 %join_channels.1 = f32[32,4,2048]{2,1,0:T(4,128)} custom-call(bf16[32,64,128]{2,1,0:T(8,128)(2,1)S(1)} %all_to_all.5.got_ref), custom_call_target="tpu_custom_call" | custom-call | tf_op jit(solution)/shard_map/join_channels/pallas_call | solution.py:188
Async XLA Ops:
  1.4 20.6 %collective-permute-start = (bf16[2,48,4,1024]{3,2,1,0:T(4,128)(2,1)S(1)}, bf16[2,48,4,1024]{3,2,1,0:T(4,128)(2,1)S(1)}, u32[]{:S(2)}, u32[]{:S(2)}) collective-permute-start(bf16[2,48,4,1024]{3,2,1,0:T(4,128)(2,1)S(1)} %slice.3), channel_id=1, source_target_pairs={{0,1},{1,2},{2,3},{4,5},{5,6},{6,7},{8,9},{9,10},{10,11},{12,13},{... | collective-permute-start | bytes 2359304 | tf_op jit(solution)/shard_map/ppermute | solution.py:148
  5.8 2.2 %copy-start = (bf16[2,256,4,1024]{3,2,1,0:T(4,128)(2,1)S(1)}, bf16[2,256,4,1024]{3,2,1,0:T(4,128)(2,1)}, u32[]{:S(2)}) copy-start(bf16[2,256,4,1024]{3,2,1,0:T(4,128)(2,1)} %volt_ref.3) | copy-start | bytes 12582916
  8.0 1.0 %copy-start.1 = (bf16[512,512]{1,0:T(8,128)(2,1)S(1)}, bf16[512,512]{1,0:T(8,128)(2,1)}, u32[]{:S(2)}) copy-start(bf16[512,512]{1,0:T(8,128)(2,1)} %constant.5.clone.table_ref) | copy-start | bytes 1572868
  9.1 0.8 %copy-start.2 = (f32[2,4,1024]{2,1,0:T(4,128)S(1)}, f32[2,4,1024]{2,1,0:T(4,128)}, u32[]{:S(2)}) copy-start(f32[2,4,1024]{2,1,0:T(4,128)} %gains_ref.3) | copy-start | bytes 98308
  9.8 0.7 %copy-start.3 = (f32[2,16,128]{2,1,0:T(8,128)S(1)}, f32[2,16,128]{2,1,0:T(8,128)}, u32[]{:S(2)}) copy-start(f32[2,16,128]{2,1,0:T(8,128)} %constant.4.clone.fine_ref) | copy-start | bytes 49156
  10.5 0.7 %copy-start.4 = (f32[64]{0:T(128)S(1)}, f32[64]{0:T(128)}, u32[]{:S(2)}) copy-start(f32[64]{0:T(128)} %param.7) | copy-start | bytes 772
where the time goes:
time: 45.7 us; the launch traced here: 45.3 us
  blocking collectives  20 us (44%)
  Pallas kernels  9.15 us (20%)
  local copies, waits for them, and re-layouts  6.76 us (15%)
  waiting for transfers between devices  4.97 us (11%)
  starting transfers between devices  4.42 us (10%)
    all_to_all x1, blocking collectives, body(): got = lax.all_to_all(power, 'freq', split_axis=0, concat_axis=0, tiled=True)  20 us
    pallas_call x1, Pallas kernels, body(): pl.pallas_call(later_kernel, grid=(TIMES,), in_specs=[pl.BlockSpec((2, SP...  5.8 us
    unnamed x10, local copies, waits for them, and re-layouts  5.35 us
    ppermute x1, waiting for transfers between devices, body(): halo = lax.ppermute(halo, 'tm', [(i, i + 1) for i in range(count - 1)])  4.97 us
    ppermute x1, starting transfers between devices, body(): halo = lax.ppermute(halo, 'tm', [(i, i + 1) for i in range(count - 1)])  4.42 us
    pallas_call x1, Pallas kernels, body(): pl.pallas_call(first_kernel, grid=(1,), in_specs=[pl.BlockSpec((2, SPAN,...  1.93 us
    pallas_call x1, Pallas kernels, body(): pl.pallas_call(join_kernel, out_shape=jax.ShapeDtypeStruct((GROUP, TIMES,...  1.42 us
    slice x1, local copies, waits for them, and re-layouts, body(): halo = voltages[:, samples - PAST:]  1.4 us
  transfers between devices with their start and end apart: 1, of which 1 were waited for; matrix products, arithmetic and copies ran while one was open for 0% of the time, Pallas kernels for 13%

commit v1 on v0

v1 whole, which is shorter than its diff:
```python
import math

import jax
import jax.numpy as jnp
import numpy as np
from jax import lax
from jax.experimental import pallas as pl
from jax.experimental.pallas import tpu as pltpu
from jax.sharding import PartitionSpec as P

EW = 4
NS = 256
FEEDS = EW * NS
FINE = 16
TAPS = 4
INTEG = 4
CHAN = 4
AHEAD = 3
SPAN = INTEG * FINE
PAST = (TAPS - 1) * FINE
GROUP = 32
HALF = 16
TIMES = 4
EARLY = TAPS - 1

F32 = jnp.float32
BF16 = jnp.bfloat16


def beam_table():
    q = np.arange(NS // 2)[:, None]
    tables = []
    scale = 1.0 / math.sqrt(NS) / math.sqrt(EW) / math.sqrt(INTEG)
    for odd in range(2):
        k = 2 * np.arange(NS // 2)[None, :] + odd
        angle = (q * k % NS).astype(np.float32) * np.float32(2.0 * math.pi / NS)
        cos = np.cos(angle).astype(jnp.bfloat16).astype(np.float32)
        sin = np.sin(angle).astype(jnp.bfloat16).astype(np.float32)
        tables.append(np.block([[cos, -sin], [sin, cos]]) * np.float32(scale))
    return np.stack(tables).astype(jnp.bfloat16)


def fill_bank(window_ref, bank_ref):
    taps = jnp.concatenate([window_ref[...], jnp.zeros((1, 64), F32)], axis=1)
    lane = lax.broadcasted_iota(jnp.int32, (1, 2 * SPAN), 1)
    line = jnp.zeros((1, 2 * SPAN), F32)
    for m in range(TAPS):
        moved = pltpu.roll(taps, (64 - 32 * m) % 128, 1)
        line = jnp.where(lane // FINE == TAPS - m, moved, line)
    f = lax.broadcasted_iota(jnp.int32, (FINE, 2 * SPAN), 0)
    n = lax.broadcasted_iota(jnp.int32, (FINE, 2 * SPAN), 1) % FINE
    turn = f * n % FINE
    scale = 1.0 / math.sqrt(FINE * TAPS)
    cos = jnp.zeros((FINE, 2 * SPAN), F32)
    sin = jnp.zeros((FINE, 2 * SPAN), F32)
    for k in range(FINE):
        angle = 2.0 * math.pi * k / FINE
        cos = jnp.where(turn == k, scale * math.cos(angle), cos)
        sin = jnp.where(turn == k, scale * math.sin(angle), sin)
    for j in range(INTEG):
        row = line if j == 0 else pltpu.roll(line, FINE * j, 1)
        re, im = (cos * row).astype(BF16), (sin * row).astype(BF16)
        bank_ref[FINE * j : FINE * (j + 1), :128] = re
        bank_ref[FINE * j : FINE * (j + 1), 128:] = im
        bank_ref[64 + FINE * j : 64 + FINE * (j + 1), :128] = -im
        bank_ref[64 + FINE * j : 64 + FINE * (j + 1), 128:] = re


def steer(spec, gr, gi):
    half = spec.shape[0] // 2
    sr, si = spec[:half], spec[half:]
    cr = gr * sr - gi * si
    ci = gr * si + gi * sr
    r0, r1, r2, r3 = (cr[:, NS * e : NS * (e + 1)] for e in range(EW))
    i0, i1, i2, i3 = (ci[:, NS * e : NS * (e + 1)] for e in range(EW))
    rs, rd, it, iu = r0 + r2, r0 - r2, i0 + i2, i0 - i2
    rv, rw, iv, iw = r1 + r3, r1 - r3, i1 + i3, i1 - i3
    return (rs + rv, it + iv), (rd + iw, iu - rw), (rs - rv, it - iv), (rd - iw, iu + rw)


def powers(bank, data_of, channels, frames, gains_ref, table_ref, left_ref):
    count = len(channels)
    rows = frames * count * FINE
    for at, c in enumerate(channels):
        spec = jnp.dot(bank, data_of(c), preferred_element_type=F32)
        beams = steer(spec, gains_ref[0, c : c + 1], gains_ref[1, c : c + 1])
        for g in range(EW):
            for part in range(2):
                low, high = beams[g][part][:, :128], beams[g][part][:, 128:]
                for odd, value in enumerate((low + high, low - high)):
                    value = value.astype(BF16)
                    lane = 256 * odd + 128 * part
                    for j in range(frames):
                        row = rows * g + FINE * (count * j + at)
                        left_ref[row : row + FINE, lane : lane + 128] = value[FINE * j : FINE * (j + 1)]
    part = rows // frames
    sums = []
    for g in range(EW):
        both = []
        for odd in range(2):
            beam = jnp.dot(
                left_ref[rows * g : rows * (g + 1), 256 * odd : 256 * (odd + 1)],
                table_ref[odd], preferred_element_type=F32,
            )
            re, im = beam[:, :128], beam[:, 128:]
            power = re * re + im * im
            total = power[:part]
            for j in range(1, frames):
                total = total + power[part * j : part * (j + 1)]
            both.append(total)
        sums.append(both)
    return sums


def by_beam(even, odd):
    power = jnp.concatenate([even, odd], axis=0)
    return power.T.astype(BF16).reshape(8, HALF, 128)


def early_bank(bank_ref):
    return jnp.concatenate([bank_ref[: FINE * EARLY], bank_ref[64 : 64 + FINE * EARLY]], axis=0)


def edge_copies(volt_ref, start, to_ref, sems):
    return [
        pltpu.make_async_copy(volt_ref.at[part, pl.ds(start, PAST)], to_ref.at[part], sems.at[part])
        for part in range(2)
    ]


def tail_kernel(volt_ref, ahead_ref, keep_ref, tail_ref, sems):
    copies = edge_copies(volt_ref, volt_ref.shape[1] - PAST, tail_ref, sems)
    for copy in copies:
        copy.start()
    for part in range(2):
        copies[part].wait()
        tail = jnp.swapaxes(tail_ref[part], 0, 1)
        ahead_ref[part] = tail[:AHEAD]
        keep_ref[part] = tail[AHEAD]


def head_kernel(volt_ref, back_ref, first_ref, head_ref, sems):
    copies = [
        pltpu.make_async_copy(volt_ref.at[part, pl.ds(0, SPAN)], head_ref.at[part], sems.at[part])
        for part in range(2)
    ]
    for copy in copies:
        copy.start()
    for part in range(2):
        copies[part].wait()
        head = jnp.swapaxes(head_ref[part], 0, 1)
        first_ref[part] = head
        back_ref[part] = head[AHEAD, :PAST]


def form_time(t, past, now_ref, gains_ref, table_ref, bank_ref, out_ref, left_ref):
    now = [jnp.swapaxes(now_ref[part], 0, 1) for part in range(2)]
    sums = powers(
        bank_ref[...],
        lambda c: jnp.concatenate([past[0][c], now[0][c], past[1][c], now[1][c]], axis=0),
        range(CHAN), INTEG, gains_ref, table_ref, left_ref,
    )
    for g in range(EW):
        out_ref[8 * g : 8 * (g + 1), HALF * t : HALF * (t + 1)] = by_beam(*sums[g])
    return now


def second_kernel(
    volt_ref, first_ref, gains_ref, table_ref, window_ref,
    out_ref, bank_ref, late_ref, second_ref, ahead_ref, block_ref, left_ref, sems,
):
    to = [block_ref] + [ahead_ref.at[i] for i in range(TIMES - 2)]
    copies = [
        pltpu.make_async_copy(volt_ref.at[:, pl.ds(SPAN * (i + 1), SPAN)], to[i], sems.at[i])
        for i in range(TIMES - 1)
    ]
    for copy in copies:
        copy.start()
    fill_bank(window_ref, bank_ref)
    sums = powers(
        jnp.concatenate([bank_ref[48:64], bank_ref[112:128]], axis=0),
        lambda c: jnp.concatenate([first_ref[0, c], first_ref[0, c], first_ref[1, c], first_ref[1, c]], axis=0),
        range(CHAN), 1, gains_ref, table_ref, left_ref,
    )
    for g in range(EW):
        for odd in range(2):
            late_ref[g, odd] = sums[g][odd]
    copies[0].wait()
    now = form_time(1, first_ref, block_ref, gains_ref, table_ref, bank_ref, out_ref, left_ref)
    for part in range(2):
        second_ref[part] = now[part]
    for copy in copies[1:]:
        copy.wait()


def later_kernel(ahead_ref, second_ref, gains_ref, table_ref, bank_ref, rest_ref, out_ref, left_ref):
    now = form_time(2, second_ref, ahead_ref.at[0], gains_ref, table_ref, bank_ref, out_ref, left_ref)
    form_time(3, now, ahead_ref.at[1], gains_ref, table_ref, bank_ref, out_ref, left_ref)


def neighbour_kernel(head_ref, keep_ref, gains_ref, table_ref, bank_ref, out_ref, left_ref):
    last = lax.axis_index("tm") == lax.axis_size("tm") - 1
    bank = early_bank(bank_ref)
    lane = lax.broadcasted_iota(jnp.int32, bank.shape, 1)
    edge = jnp.where(last, SPAN, 0)
    bank = jnp.where(lane % 128 < edge, 0.0, bank.astype(F32)).astype(BF16)
    pad = jnp.zeros((SPAN - PAST, FEEDS), BF16)
    sums = powers(
        bank,
        lambda c: jnp.concatenate(
            [pad, keep_ref[0], head_ref[0], pad, pad, keep_ref[1], head_ref[1], pad], axis=0
        ),
        (AHEAD,), EARLY, gains_ref, table_ref, left_ref,
    )
    for g in range(EW):
        for odd in range(2):
            out_ref[g, odd] = sums[g][odd].astype(BF16)


def first_kernel(
    halo_ref, now_ref, back_ref, late_ref, gains_ref, table_ref, bank_ref, rest_ref, out_ref, left_ref
):
    pad = jnp.zeros((SPAN - PAST, FEEDS), BF16)
    sums = powers(
        early_bank(bank_ref),
        lambda c: jnp.concatenate(
            [pad, halo_ref[0, c], now_ref[0, c], pad, halo_ref[1, c], now_ref[1, c]], axis=0
        ),
        range(AHEAD), EARLY, gains_ref, table_ref, left_ref,
    )
    for g in range(EW):
        power = [
            late_ref[g, odd] + jnp.concatenate([sums[g][odd], back_ref[g, odd].astype(F32)], axis=0)
            for odd in range(2)
        ]
        out_ref[8 * g : 8 * (g + 1), :HALF] = by_beam(*power)


def join_kernel(got_ref, out_ref, joined_ref, sems):
    lane = lax.broadcasted_iota(jnp.int32, (1, 128), 1)
    low = lane < 64
    chunks = joined_ref.shape[0]
    pairs = GROUP // 2 // chunks
    copies = []
    for i in range(chunks):
        for p in range(pairs):
            s = pairs * i + p
            a = got_ref[2 * s].astype(F32)
            b = got_ref[2 * s + 1].astype(F32)
            first = jnp.where(low, a, pltpu.roll(b, 64, 1)).reshape(TIMES, HALF, 128)
            second = jnp.where(low, pltpu.roll(a, 64, 1), b).reshape(TIMES, HALF, 128)
            joined_ref[i, :, 0, :, 128 * p : 128 * (p + 1)] = jnp.swapaxes(first, 0, 1)
            joined_ref[i, :, 1, :, 128 * p : 128 * (p + 1)] = jnp.swapaxes(second, 0, 1)
        width = 128 * pairs
        copy = pltpu.make_async_copy(
            joined_ref.at[i], out_ref.at[:, :, :, pl.ds(width * i, width)], sems.at[i]
        )
        copy.start()
        copies.append(copy)
    for copy in copies:
        copy.wait()


def params(mib):
    return pltpu.CompilerParams(vmem_limit_bytes=mib << 20)


def cost(rows, moved):
    return pl.CostEstimate(flops=2 * rows * 512 * 512, bytes_accessed=moved, transcendentals=0)


VMEM = pl.BlockSpec(memory_space=pltpu.VMEM)
HBM = pl.BlockSpec(memory_space=pltpu.HBM)


def body(voltages, gains, window):
    count = lax.axis_size("tm")
    table = jnp.asarray(beam_table())

    window = window.reshape(1, FINE * TAPS)
    edge_scratch = [pltpu.VMEM((2, PAST, CHAN, FEEDS), BF16), pltpu.SemaphoreType.DMA((2,))]
    ahead, keep = pl.pallas_call(
        tail_kernel,
        in_specs=[HBM],
        out_specs=[VMEM] * 2,
        out_shape=[
            jax.ShapeDtypeStruct((2, AHEAD, PAST, FEEDS), BF16),
            jax.ShapeDtypeStruct((2, PAST, FEEDS), BF16),
        ],
        scratch_shapes=edge_scratch,
        compiler_params=params(51),
        name="block_tail",
    )(voltages)
    forward = [(i, (i + 1) % count) for i in range(count)]
    backward = [((i + 1) % count, i) for i in range(count)]
    halo = lax.ppermute(ahead, "tm", forward[:-1])
    back, first = pl.pallas_call(
        head_kernel,
        in_specs=[HBM],
        out_specs=[VMEM] * 2,
        out_shape=[
            jax.ShapeDtypeStruct((2, PAST, FEEDS), BF16),
            jax.ShapeDtypeStruct((2, CHAN, SPAN, FEEDS), BF16),
        ],
        scratch_shapes=[pltpu.VMEM((2, SPAN, CHAN, FEEDS), BF16), pltpu.SemaphoreType.DMA((2,))],
        compiler_params=params(46),
        name="block_head",
    )(voltages)
    head = lax.ppermute(back, "tm", backward)

    power_shape = jax.ShapeDtypeStruct((GROUP, TIMES * HALF, 128), BF16)
    rest, bank, late, second, blocks = pl.pallas_call(
        second_kernel,
        in_specs=[HBM] + [VMEM] * 4,
        out_specs=[VMEM] * 5,
        out_shape=[
            power_shape,
            jax.ShapeDtypeStruct((128, 256), BF16),
            jax.ShapeDtypeStruct((EW, 2, SPAN, NS // 2), F32),
            jax.ShapeDtypeStruct((2, CHAN, SPAN, FEEDS), BF16),
            jax.ShapeDtypeStruct((TIMES - 2, 2, SPAN, CHAN, FEEDS), BF16),
        ],
        scratch_shapes=[
            pltpu.VMEM((2, SPAN, CHAN, FEEDS), BF16),
            pltpu.VMEM((1024, 512), BF16),
            pltpu.SemaphoreType.DMA((TIMES - 1,)),
        ],
        compiler_params=params(42),
        cost_estimate=cost(1280, 4 << 20),
        name="second_time",
    )(voltages, first, gains, table, window)
    rest = pl.pallas_call(
        later_kernel,
        in_specs=[VMEM] * 6,
        out_specs=VMEM,
        out_shape=power_shape,
        scratch_shapes=[pltpu.VMEM((1024, 512), BF16)],
        input_output_aliases={5: 0},
        compiler_params=params(24),
        cost_estimate=cost(2048, 4 << 20),
        name="later_times",
    )(blocks, second, gains, table, bank, rest)
    keep, rest = lax.optimization_barrier((keep, rest))
    returned = pl.pallas_call(
        neighbour_kernel,
        in_specs=[VMEM] * 5,
        out_specs=VMEM,
        out_shape=jax.ShapeDtypeStruct((EW, 2, FINE, NS // 2), BF16),
        scratch_shapes=[pltpu.VMEM((192, 512), BF16)],
        compiler_params=params(16),
        cost_estimate=cost(192, 1 << 20),
        name="next_block",
    )(head, keep, gains, table, bank)
    returned = lax.ppermute(returned, "tm", forward)
    power = pl.pallas_call(
        first_kernel,
        in_specs=[VMEM] * 8,
        out_specs=VMEM,
        out_shape=power_shape,
        scratch_shapes=[pltpu.VMEM((576, 512), BF16)],
        input_output_aliases={7: 0},
        compiler_params=params(24),
        cost_estimate=cost(576, 3 << 20),
        name="first_time",
    )(halo, first, returned, late, gains, table, bank, rest)
    got = lax.all_to_all(power, "freq", split_axis=0, concat_axis=0, tiled=True)
    chunks = 4
    wide = GROUP * CHAN * FINE
    joined = pl.pallas_call(
        join_kernel,
        in_specs=[VMEM],
        out_specs=HBM,
        out_shape=jax.ShapeDtypeStruct((HALF, 2, TIMES, wide), F32),
        scratch_shapes=[
            pltpu.VMEM((chunks, HALF, 2, TIMES, wide // chunks), F32),
            pltpu.SemaphoreType.DMA((chunks,)),
        ],
        compiler_params=params(16),
        name="join_channels",
    )(got)
    return joined.reshape(GROUP, TIMES, wide)


def solution(mesh):
    placed = (P(None, "tm", "freq", None), P(None, "freq", None), P())
    return jax.shard_map(
        body, mesh=mesh, in_specs=placed, out_specs=P("freq", "tm", None), check_vma=False
    )
```

time: 45.7 us -> 40.8 us (0.89)
  local copies, waits for them, and re-layouts: 6.76 us -> 0.02 us
  starting transfers between devices: 4.42 us -> 6.32 us
  Pallas kernels: 9.15 us -> 9.93 us
  waiting for transfers between devices: 4.97 us -> 4.38 us
    unnamed x10 -> x8, local copies, waits for them, and re-layouts: 5.35 us -> 0.02 us
    ppermute x1 -> x3, starting transfers between devices: 4.42 us -> 6.32 us  [the longest x1 4.54 us: body(): halo = lax.ppermute(ahead, 'tm', forward[:-1])]
    slice x1 -> x0, local copies, waits for them, and re-layouts: 1.4 us -> none  [body(): halo = voltages[:, samples - PAST:]]
    pallas_call x3 -> x7, Pallas kernels: 9.15 us -> 9.93 us  [the longest x1 2.95 us: body(): pl.pallas_call(later_kernel, in_specs=[VMEM] * 6, out_specs=VMEM, out_sha...]
    ppermute x1 -> x3, waiting for transfers between devices: 4.97 us -> 4.38 us  [the longest x1 4.37 us: body(): returned = lax.ppermute(returned, 'tm', forward)]
  transfers between devices with their start and end apart: 1 -> 3, of which waited for: 1 -> 1; matrix products, arithmetic and copies ran while one was open for 0% -> 0% of each run, Pallas kernels for 13% -> 16%
where the time goes in v1:
time: 40.8 us; the launch traced here: 40.7 us
  blocking collectives  20 us (49%)
  Pallas kernels  9.93 us (24%)
  starting transfers between devices  6.32 us (15%)
  waiting for transfers between devices  4.38 us (11%)
    all_to_all x1, blocking collectives, body(): got = lax.all_to_all(power, 'freq', split_axis=0, concat_axis=0, tiled=True)  20 us
    ppermute x1, starting transfers between devices, body(): halo = lax.ppermute(ahead, 'tm', forward[:-1])  4.54 us
    ppermute x1, waiting for transfers between devices, body(): returned = lax.ppermute(returned, 'tm', forward)  4.37 us
    pallas_call x1, Pallas kernels, body(): pl.pallas_call(later_kernel, in_specs=[VMEM] * 6, out_specs=VMEM, out_sha...  2.95 us
    pallas_call x1, Pallas kernels, body(): pl.pallas_call(second_kernel, in_specs=[HBM] + [VMEM] * 4, out_specs=[VME...  2.63 us
    ppermute x1, starting transfers between devices, body(): head = lax.ppermute(back, 'tm', backward)  1.54 us
    pallas_call x1, Pallas kernels, body(): pl.pallas_call(tail_kernel, in_specs=[HBM], out_specs=[VMEM] * 2, out_sha...  1.38 us
    pallas_call x1, Pallas kernels, body(): pl.pallas_call(join_kernel, in_specs=[VMEM], out_specs=HBM, out_shape=jax...  1.19 us
  transfers between devices with their start and end apart: 3, of which 1 were waited for; matrix products, arithmetic and copies ran while one was open for 0% of the time, Pallas kernels for 16%

profile of v1, /device:TPU:1, one launch (start us, length us, event | category | flops | bytes accessed | tf_op | source)
XLA Modules:
  0.0 40.7 jit_solution(1704388238078751232)
XLA Ops:
  0.0 0.0 copy-start
  0.0 0.0 copy-start.1
  0.0 0.0 copy-start.3
  0.0 0.0 copy-start.2
  0.0 1.4 %block_tail.1 = (bf16[2,3,48,1024]{3,2,1,0:T(8,128)(2,1)S(1)}, bf16[2,48,1024]{2,1,0:T(8,128)(2,1)S(1)}) custom-call(bf16[2,256,4,1024]{3,2,1,0:T(4,128)(2,1)} %volt_ref.5), custom_call_target="tpu_custom_call" | custom-call | tf_op jit(solution)/shard_map/block_tail/pallas_call | solution.py:282
  1.4 4.5 %collective-permute-start = (bf16[2,3,48,1024]{3,2,1,0:T(8,128)(2,1)S(1)}, bf16[2,3,48,1024]{3,2,1,0:T(8,128)(2,1)S(1)}, u32[]{:S(2)}, u32[]{:S(2)}) collective-permute-start(bf16[2,3,48,1024]{3,2,1,0:T(8,128)(2,1)S(1)} %get-tuple-element.16), channel_id=1, source_target_pairs={{0,1},{1,2},{2,3},{4,5},{5,6},{6,7},{8,9},{9,10},{10,11},{12,13},{... | collective-permute-start | bytes 1769480 | tf_op jit(solution)/shard_map/ppermute | solution.py:296
  6.0 0.0 copy-done
  6.0 0.4 block_head.1
  6.3 1.5 %collective-permute-start.1 = (bf16[2,48,1024]{2,1,0:T(8,128)(2,1)S(1)}, bf16[2,48,1024]{2,1,0:T(8,128)(2,1)S(1)}, u32[]{:S(2)}, u32[]{:S(2)}) collective-permute-start(bf16[2,48,1024]{2,1,0:T(8,128)(2,1)S(1)} %get-tuple-element.18), channel_id=1, source_target_pairs={{1,0},{2,1},{3,2},{0,3},{5,4},{6,5},{7,6},{4,7},{9,8},{10,9},{11,1... | collective-permute-start | bytes 589832 | tf_op jit(solution)/shard_map/ppermute | solution.py:309
  7.9 0.0 copy-done.1
  7.9 0.0 copy-done.3
  7.9 0.0 copy-done.2
  7.9 2.6 %second_time.1 = (bf16[32,64,128]{2,1,0:T(8,128)(2,1)S(1)}, bf16[128,256]{1,0:T(8,128)(2,1)S(1)}, f32[4,2,64,128]{3,2,1,0:T(8,128)S(1)}, bf16[2,4,64,1024]{3,2,1...) custom-call(bf16[2,256,4,1024]{3,2,1,0:T(4,128)(2,1)S(1)} %copy-done, ...), custom_call_target="tpu_custom_call" | custom-call | flops 671088640 | bytes 4194304 | tf_op jit(solution)/shard_map/second_time/pallas_call | solution.py:312
  10.5 2.9 %later_times.1.rest_ref = bf16[32,64,128]{2,1,0:T(8,128)(2,1)S(1)} custom-call(bf16[2,2,64,4,1024]{4,3,2,1,0:T(4,128)(2,1)S(1)} %get-tuple-element.20.ahead_ref, bf16[2,4,64,1024]{3,2,1,0:T(8,128)(2,1)S(1)} %get-tuple-element.21.second_ref, f32[2,4,1024]{2,1,0:T(4,128)S(1)} %copy-done.2, ...), custom_call_target="tpu_custom_call", output_to_operand_aliasing={{}: (5, {})} | custom-call | flops 1073741824 | bytes 4194304 | tf_op jit(solution)/shard_map/later_times/pallas_call | solution.py:332
  13.5 0.0 collective-permute-done.1.head_ref
  13.5 0.5 %next_block.1 = bf16[4,2,16,128]{3,2,1,0:T(8,128)(2,1)S(1)} custom-call(bf16[2,48,1024]{2,1,0:T(8,128)(2,1)S(1)} %collective-permute-done.1.head_ref, bf16[2,48,1024]{2,1,0:T(8,128)(2,1)S(1)} %get-tuple-element.24.keep_ref, f32[2,4,1024]{2,1,0:T(4,128)S(1)} %copy-done.2, bf16[2,256,256]{2,1,0:T(8,128)(2,1)S(1)} %copy-done.1, ...), custom_call_target="tpu_custom_call" | custom-call | flops 100663296 | bytes 1048576 | tf_op jit(solution)/shard_map/next_block/pallas_call | solution.py:344
  14.0 0.2 collective-permute-start.2
  14.2 4.4 %collective-permute-done.2.back_ref = bf16[4,2,16,128]{3,2,1,0:T(8,128)(2,1)S(1)} collective-permute-done((bf16[4,2,16,128]{3,2,1,0:T(8,128)(2,1)S(1)}, bf16[4,2,16,128]{3,2,1,0:T(8,128)(2,1)S(1)}, u32[]{:S(2)}, u32[]{:S(2)}) %collective-permute-start.2) | collective-permute-done | bytes 32800 | tf_op jit(solution)/shard_map/ppermute | solution.py:354
  18.6 0.0 collective-permute-done.halo_ref
  18.6 0.9 %first_time.1 = bf16[32,64,128]{2,1,0:T(8,128)(2,1)S(1)} custom-call(bf16[2,3,48,1024]{3,2,1,0:T(8,128)(2,1)S(1)} %collective-permute-done.halo_ref, bf16[2,4,64,1024]{3,2,1,0:T(8,128)(2,1)S(1)} %get-tuple-element.17.first_ref.now_ref, bf16[4,2,16,128]{3,2,1,0:T(8,128)(2,1)S(1)} %collective-permute-done.2.back_ref, ...), custom_call_target="tpu_custom_call", output_to_operand_aliasing={{}: (7, {})} | custom-call | flops 301989888 | bytes 3145728 | tf_op jit(solution)/shard_map/first_time/pallas_call | solution.py:355
  19.5 20.0 %all_to_all.5.got_ref = bf16[32,64,128]{2,1,0:T(8,128)(2,1)S(1)} all-to-all(bf16[32,64,128]{2,1,0:T(8,128)(2,1)S(1)} %first_time.1), channel_id=1, replica_groups=mesh['freq'=32,'tm'=4] {'freq'}, dimensions={0} | all-to-all | bytes 1048576 | tf_op jit(solution)/shard_map/all_to_all | solution.py:366
  39.5 1.2 %join_channels.1 = f32[16,2,4,2048]{3,2,1,0:T(4,128)} custom-call(bf16[32,64,128]{2,1,0:T(8,128)(2,1)S(1)} %all_to_all.5.got_ref), custom_call_target="tpu_custom_call" | custom-call | tf_op jit(solution)/shard_map/join_channels/pallas_call | solution.py:369
Async XLA Ops:
  0.0 6.0 %copy-start = (bf16[2,256,4,1024]{3,2,1,0:T(4,128)(2,1)S(1)}, bf16[2,256,4,1024]{3,2,1,0:T(4,128)(2,1)}, u32[]{:S(2)}) copy-start(bf16[2,256,4,1024]{3,2,1,0:T(4,128)(2,1)} %volt_ref.5) | copy-start | bytes 12582916
  0.0 7.9 %copy-start.1 = (bf16[2,256,256]{2,1,0:T(8,128)(2,1)S(1)}, bf16[2,256,256]{2,1,0:T(8,128)(2,1)}, u32[]{:S(2)}) copy-start(bf16[2,256,256]{2,1,0:T(8,128)(2,1)} %constant.2.clone.table_ref) | copy-start | bytes 786436
  0.0 7.9 %copy-start.3 = (f32[64]{0:T(128)S(1)}, f32[64]{0:T(128)}, u32[]{:S(2)}) copy-start(f32[64]{0:T(128)} %param.6) | copy-start | bytes 772
  0.0 7.9 %copy-start.2 = (f32[2,4,1024]{2,1,0:T(4,128)S(1)}, f32[2,4,1024]{2,1,0:T(4,128)}, u32[]{:S(2)}) copy-start(f32[2,4,1024]{2,1,0:T(4,128)} %gains_ref.7) | copy-start | bytes 98308
  1.4 17.2 %collective-permute-start = (bf16[2,3,48,1024]{3,2,1,0:T(8,128)(2,1)S(1)}, bf16[2,3,48,1024]{3,2,1,0:T(8,128)(2,1)S(1)}, u32[]{:S(2)}, u32[]{:S(2)}) collective-permute-start(bf16[2,3,48,1024]{3,2,1,0:T(8,128)(2,1)S(1)} %get-tuple-element.16), channel_id=1, source_target_pairs={{0,1},{1,2},{2,3},{4,5},{5,6},{6,7},{8,9},{9,10},{10,11},{12,13},{... | collective-permute-start | bytes 1769480 | tf_op jit(solution)/shard_map/ppermute | solution.py:296
  6.3 7.1 %collective-permute-start.1 = (bf16[2,48,1024]{2,1,0:T(8,128)(2,1)S(1)}, bf16[2,48,1024]{2,1,0:T(8,128)(2,1)S(1)}, u32[]{:S(2)}, u32[]{:S(2)}) collective-permute-start(bf16[2,48,1024]{2,1,0:T(8,128)(2,1)S(1)} %get-tuple-element.18), channel_id=1, source_target_pairs={{1,0},{2,1},{3,2},{0,3},{5,4},{6,5},{7,6},{4,7},{9,8},{10,9},{11,1... | collective-permute-start | bytes 589832 | tf_op jit(solution)/shard_map/ppermute | solution.py:309
  14.0 4.6 %collective-permute-start.2 = (bf16[4,2,16,128]{3,2,1,0:T(8,128)(2,1)S(1)}, bf16[4,2,16,128]{3,2,1,0:T(8,128)(2,1)S(1)}, u32[]{:S(2)}, u32[]{:S(2)}) collective-permute-start(bf16[4,2,16,128]{3,2,1,0:T(8,128)(2,1)S(1)} %next_block.1), channel_id=1, source_target_pairs={{0,1},{1,2},{2,3},{3,0},{4,5},{5,6},{6,7},{7,4},{8,9},{9,10},{10,1... | collective-permute-start | bytes 98312 | tf_op jit(solution)/shard_map/ppermute | solution.py:354

commit v2 on v1

--- a/solution.py
+++ b/solution.py
@@ -94,21 +94,21 @@
                         row = rows * g + FINE * (count * j + at)
                         left_ref[row : row + FINE, lane : lane + 128] = value[FINE * j : FINE * (j + 1)]
     part = rows // frames
-    sums = []
-    for g in range(EW):
-        both = []
+    step = EW if rows < 256 else 1
+    sums = [[None, None] for _ in range(EW)]
+    for g in range(0, EW, step):
         for odd in range(2):
             beam = jnp.dot(
-                left_ref[rows * g : rows * (g + 1), 256 * odd : 256 * (odd + 1)],
+                left_ref[rows * g : rows * (g + step), 256 * odd : 256 * (odd + 1)],
                 table_ref[odd], preferred_element_type=F32,
             )
             re, im = beam[:, :128], beam[:, 128:]
             power = re * re + im * im
-            total = power[:part]
-            for j in range(1, frames):
-                total = total + power[part * j : part * (j + 1)]
-            both.append(total)
-        sums.append(both)
+            for i in range(step):
+                total = power[rows * i : rows * i + part]
+                for j in range(1, frames):
+                    total = total + power[rows * i + part * j : rows * i + part * (j + 1)]
+                sums[g + i][odd] = total
     return sums
 
 
@@ -121,22 +121,17 @@
     return jnp.concatenate([bank_ref[: FINE * EARLY], bank_ref[64 : 64 + FINE * EARLY]], axis=0)
 
 
-def edge_copies(volt_ref, start, to_ref, sems):
-    return [
-        pltpu.make_async_copy(volt_ref.at[part, pl.ds(start, PAST)], to_ref.at[part], sems.at[part])
+def tail_kernel(volt_ref, ahead_ref, tail_ref, sems):
+    start = volt_ref.shape[1] - PAST
+    copies = [
+        pltpu.make_async_copy(volt_ref.at[part, pl.ds(start, PAST)], tail_ref.at[part], sems.at[part])
         for part in range(2)
     ]
-
-
-def tail_kernel(volt_ref, ahead_ref, keep_ref, tail_ref, sems):
-    copies = edge_copies(volt_ref, volt_ref.shape[1] - PAST, tail_ref, sems)
     for copy in copies:
         copy.start()
     for part in range(2):
         copies[part].wait()
-        tail = jnp.swapaxes(tail_ref[part], 0, 1)
-        ahead_ref[part] = tail[:AHEAD]
-        keep_ref[part] = tail[AHEAD]
+        ahead_ref[part] = jnp.swapaxes(tail_ref[part], 0, 1)[:AHEAD]
 
 
 def head_kernel(volt_ref, back_ref, first_ref, head_ref, sems):
@@ -153,7 +148,7 @@
         back_ref[part] = head[AHEAD, :PAST]
 
 
-def form_time(t, past, now_ref, gains_ref, table_ref, bank_ref, out_ref, left_ref):
+def form_time(at, past, now_ref, gains_ref, table_ref, bank_ref, out_ref, left_ref):
     now = [jnp.swapaxes(now_ref[part], 0, 1) for part in range(2)]
     sums = powers(
         bank_ref[...],
@@ -161,7 +156,7 @@
         range(CHAN), INTEG, gains_ref, table_ref, left_ref,
     )
     for g in range(EW):
-        out_ref[8 * g : 8 * (g + 1), HALF * t : HALF * (t + 1)] = by_beam(*sums[g])
+        out_ref[8 * g : 8 * (g + 1), HALF * at : HALF * (at + 1)] = by_beam(*sums[g])
     return now
 
 
@@ -186,16 +181,18 @@
         for odd in range(2):
             late_ref[g, odd] = sums[g][odd]
     copies[0].wait()
-    now = form_time(1, first_ref, block_ref, gains_ref, table_ref, bank_ref, out_ref, left_ref)
+    now = form_time(0, first_ref, block_ref, gains_ref, table_ref, bank_ref, out_ref, left_ref)
     for part in range(2):
         second_ref[part] = now[part]
     for copy in copies[1:]:
         copy.wait()
 
 
-def later_kernel(ahead_ref, second_ref, gains_ref, table_ref, bank_ref, rest_ref, out_ref, left_ref):
-    now = form_time(2, second_ref, ahead_ref.at[0], gains_ref, table_ref, bank_ref, out_ref, left_ref)
-    form_time(3, now, ahead_ref.at[1], gains_ref, table_ref, bank_ref, out_ref, left_ref)
+def later_kernel(ahead_ref, second_ref, gains_ref, table_ref, bank_ref, out_ref, keep_ref, left_ref):
+    now = form_time(0, second_ref, ahead_ref.at[0], gains_ref, table_ref, bank_ref, out_ref, left_ref)
+    now = form_time(1, now, ahead_ref.at[1], gains_ref, table_ref, bank_ref, out_ref, left_ref)
+    for part in range(2):
+        keep_ref[part] = now[part][AHEAD, SPAN - PAST :]
 
 
 def neighbour_kernel(head_ref, keep_ref, gains_ref, table_ref, bank_ref, out_ref, left_ref):
@@ -218,8 +215,11 @@
 
 
 def first_kernel(
-    halo_ref, now_ref, back_ref, late_ref, gains_ref, table_ref, bank_ref, rest_ref, out_ref, left_ref
+    halo_ref, now_ref, back_ref, late_ref, gains_ref, table_ref, bank_ref, second_ref, later_ref,
+    out_ref, left_ref,
 ):
+    out_ref[:, HALF : 2 * HALF] = second_ref[...]
+    out_ref[:, 2 * HALF :] = later_ref[...]
     pad = jnp.zeros((SPAN - PAST, FEEDS), BF16)
     sums = powers(
         early_bank(bank_ref),
@@ -278,16 +278,12 @@
     table = jnp.asarray(beam_table())
 
     window = window.reshape(1, FINE * TAPS)
-    edge_scratch = [pltpu.VMEM((2, PAST, CHAN, FEEDS), BF16), pltpu.SemaphoreType.DMA((2,))]
-    ahead, keep = pl.pallas_call(
+    ahead = pl.pallas_call(
         tail_kernel,
         in_specs=[HBM],
-        out_specs=[VMEM] * 2,
-        out_shape=[
-            jax.ShapeDtypeStruct((2, AHEAD, PAST, FEEDS), BF16),
-            jax.ShapeDtypeStruct((2, PAST, FEEDS), BF16),
-        ],
-        scratch_shapes=edge_scratch,
+        out_specs=VMEM,
+        out_shape=jax.ShapeDtypeStruct((2, AHEAD, PAST, FEEDS), BF16),
+        scratch_shapes=[pltpu.VMEM((2, PAST, CHAN, FEEDS), BF16), pltpu.SemaphoreType.DMA((2,))],
         compiler_params=params(51),
         name="block_tail",
     )(voltages)
@@ -308,13 +304,15 @@
     )(voltages)
     head = lax.ppermute(back, "tm", backward)
 
-    power_shape = jax.ShapeDtypeStruct((GROUP, TIMES * HALF, 128), BF16)
-    rest, bank, late, second, blocks = pl.pallas_call(
+    def powers_of(times):
+        return jax.ShapeDtypeStruct((GROUP, times * HALF, 128), BF16)
+
+    power_1, bank, late, second, blocks = pl.pallas_call(
         second_kernel,
         in_specs=[HBM] + [VMEM] * 4,
         out_specs=[VMEM] * 5,
         out_shape=[
-            power_shape,
+            powers_of(1),
             jax.ShapeDtypeStruct((128, 256), BF16),
             jax.ShapeDtypeStruct((EW, 2, SPAN, NS // 2), F32),
             jax.ShapeDtypeStruct((2, CHAN, SPAN, FEEDS), BF16),
@@ -329,18 +327,16 @@
         cost_estimate=cost(1280, 4 << 20),
         name="second_time",
     )(voltages, first, gains, table, window)
-    rest = pl.pallas_call(
+    power_23, keep = pl.pallas_call(
         later_kernel,
-        in_specs=[VMEM] * 6,
-        out_specs=VMEM,
-        out_shape=power_shape,
+        in_specs=[VMEM] * 5,
+        out_specs=[VMEM] * 2,
+        out_shape=[powers_of(TIMES - 2), jax.ShapeDtypeStruct((2, PAST, FEEDS), BF16)],
         scratch_shapes=[pltpu.VMEM((1024, 512), BF16)],
-        input_output_aliases={5: 0},
         compiler_params=params(24),
         cost_estimate=cost(2048, 4 << 20),
         name="later_times",
-    )(blocks, second, gains, table, bank, rest)
-    keep, rest = lax.optimization_barrier((keep, rest))
+    )(blocks, second, gains, table, bank)
     returned = pl.pallas_call(
         neighbour_kernel,
         in_specs=[VMEM] * 5,
@@ -354,17 +350,16 @@
     returned = lax.ppermute(returned, "tm", forward)
     power = pl.pallas_call(
         first_kernel,
-        in_specs=[VMEM] * 8,
+        in_specs=[VMEM] * 9,
         out_specs=VMEM,
-        out_shape=power_shape,
+        out_shape=powers_of(TIMES),
         scratch_shapes=[pltpu.VMEM((576, 512), BF16)],
-        input_output_aliases={7: 0},
         compiler_params=params(24),
         cost_estimate=cost(576, 3 << 20),
         name="first_time",
-    )(halo, first, returned, late, gains, table, bank, rest)
+    )(halo, first, returned, late, gains, table, bank, power_1, power_23)
     got = lax.all_to_all(power, "freq", split_axis=0, concat_axis=0, tiled=True)
-    chunks = 4
+    chunks = 8
     wide = GROUP * CHAN * FINE
     joined = pl.pallas_call(
         join_kernel,

time: 40.8 us -> 40.8 us (level)
  no operation moved by 1% of the time
where the time goes in v2:
time: 40.8 us; the launch traced here: 40.6 us
  blocking collectives  20 us (49%)
  Pallas kernels  9.77 us (24%)
  starting transfers between devices  6.32 us (15%)
  waiting for transfers between devices  4.48 us (11%)
    all_to_all x1, blocking collectives, body(): got = lax.all_to_all(power, 'freq', split_axis=0, concat_axis=0, tiled=True)  20 us
    ppermute x1, starting transfers between devices, body(): halo = lax.ppermute(ahead, 'tm', forward[:-1])  4.54 us
    ppermute x1, waiting for transfers between devices, body(): returned = lax.ppermute(returned, 'tm', forward)  4.47 us
    pallas_call x1, Pallas kernels, body(): pl.pallas_call(later_kernel, in_specs=[VMEM] * 5, out_specs=[VMEM] * 2, o...  2.95 us
    pallas_call x1, Pallas kernels, body(): pl.pallas_call(second_kernel, in_specs=[HBM] + [VMEM] * 4, out_specs=[VME...  2.59 us
    ppermute x1, starting transfers between devices, body(): head = lax.ppermute(back, 'tm', backward)  1.54 us
    pallas_call x1, Pallas kernels, body(): pl.pallas_call(tail_kernel, in_specs=[HBM], out_specs=VMEM, out_shape=jax...  1.36 us
    pallas_call x1, Pallas kernels, body(): pl.pallas_call(join_kernel, in_specs=[VMEM], out_specs=HBM, out_shape=jax...  1.14 us
  transfers between devices with their start and end apart: 3, of which 1 were waited for; matrix products, arithmetic and copies ran while one was open for 0% of the time, Pallas kernels for 16%

profile of v2, /device:TPU:1, one launch (start us, length us, event | category | flops | bytes accessed | tf_op | source)
XLA Modules:
  0.0 40.6 jit_solution(6849138367571377541)
XLA Ops:
  0.0 0.0 copy-start.1
  0.0 0.0 copy-start
  0.0 0.0 copy-start.3
  0.0 0.0 copy-start.2
  0.0 1.4 %block_tail.1 = bf16[2,3,48,1024]{3,2,1,0:T(8,128)(2,1)S(1)} custom-call(bf16[2,256,4,1024]{3,2,1,0:T(4,128)(2,1)} %volt_ref.5), custom_call_target="tpu_custom_call" | custom-call | tf_op jit(solution)/shard_map/block_tail/pallas_call | solution.py:281
  1.4 4.5 %collective-permute-start = (bf16[2,3,48,1024]{3,2,1,0:T(8,128)(2,1)S(1)}, bf16[2,3,48,1024]{3,2,1,0:T(8,128)(2,1)S(1)}, u32[]{:S(2)}, u32[]{:S(2)}) collective-permute-start(bf16[2,3,48,1024]{3,2,1,0:T(8,128)(2,1)S(1)} %block_tail.1), channel_id=1, source_target_pairs={{0,1},{1,2},{2,3},{4,5},{5,6},{6,7},{8,9},{9,10},{10,11},{12,13},{... | collective-permute-start | bytes 1769480 | tf_op jit(solution)/shard_map/ppermute | solution.py:292
  5.9 0.0 copy-done
  5.9 0.4 block_head.1
  6.3 1.5 %collective-permute-start.1 = (bf16[2,48,1024]{2,1,0:T(8,128)(2,1)S(1)}, bf16[2,48,1024]{2,1,0:T(8,128)(2,1)S(1)}, u32[]{:S(2)}, u32[]{:S(2)}) collective-permute-start(bf16[2,48,1024]{2,1,0:T(8,128)(2,1)S(1)} %get-tuple-element.15), channel_id=1, source_target_pairs={{1,0},{2,1},{3,2},{0,3},{5,4},{6,5},{7,6},{4,7},{9,8},{10,9},{11,1... | collective-permute-start | bytes 589832 | tf_op jit(solution)/shard_map/ppermute | solution.py:305
  7.8 0.0 copy-done.1
  7.9 0.0 copy-done.3
  7.9 0.0 copy-done.2
  7.9 2.6 %second_time.1 = (bf16[32,16,128]{2,1,0:T(8,128)(2,1)S(1)}, bf16[128,256]{1,0:T(8,128)(2,1)S(1)}, f32[4,2,64,128]{3,2,1,0:T(8,128)S(1)}, bf16[2,4,64,1024]{3,2,1...) custom-call(bf16[2,256,4,1024]{3,2,1,0:T(4,128)(2,1)S(1)} %copy-done, ...), custom_call_target="tpu_custom_call" | custom-call | flops 671088640 | bytes 4194304 | tf_op jit(solution)/shard_map/second_time/pallas_call | solution.py:310
  10.5 2.9 %later_times.1 = (bf16[32,32,128]{2,1,0:T(8,128)(2,1)S(1)}, bf16[2,48,1024]{2,1,0:T(8,128)(2,1)S(1)}) custom-call(bf16[2,2,64,4,1024]{4,3,2,1,0:T(4,128)(2,1)S(1)} %get-tuple-element.16.ahead_ref, bf16[2,4,64,1024]{3,2,1,0:T(8,128)(2,1)S(1)} %get-tuple-element.17.second_ref, f32[2,4,1024]{2,1,0:T(4,128)S(1)} %copy-done.2, ...), custom_call_target="tpu_custom_call" | custom-call | flops 1073741824 | bytes 4194304 | tf_op jit(solution)/shard_map/later_times/pallas_call | solution.py:330
  13.4 0.0 collective-permute-done.1.head_ref
  13.4 0.4 %next_block.1 = bf16[4,2,16,128]{3,2,1,0:T(8,128)(2,1)S(1)} custom-call(bf16[2,48,1024]{2,1,0:T(8,128)(2,1)S(1)} %collective-permute-done.1.head_ref, bf16[2,48,1024]{2,1,0:T(8,128)(2,1)S(1)} %get-tuple-element.19.keep_ref, f32[2,4,1024]{2,1,0:T(4,128)S(1)} %copy-done.2, bf16[2,256,256]{2,1,0:T(8,128)(2,1)S(1)} %copy-done.1, ...), custom_call_target="tpu_custom_call" | custom-call | flops 100663296 | bytes 1048576 | tf_op jit(solution)/shard_map/next_block/pallas_call | solution.py:340
  13.9 0.2 collective-permute-start.2
  14.1 4.5 %collective-permute-done.2.back_ref = bf16[4,2,16,128]{3,2,1,0:T(8,128)(2,1)S(1)} collective-permute-done((bf16[4,2,16,128]{3,2,1,0:T(8,128)(2,1)S(1)}, bf16[4,2,16,128]{3,2,1,0:T(8,128)(2,1)S(1)}, u32[]{:S(2)}, u32[]{:S(2)}) %collective-permute-start.2) | collective-permute-done | bytes 32800 | tf_op jit(solution)/shard_map/ppermute | solution.py:350
  18.6 0.0 collective-permute-done.halo_ref
  18.6 0.9 %first_time.1 = bf16[32,64,128]{2,1,0:T(8,128)(2,1)S(1)} custom-call(bf16[2,3,48,1024]{3,2,1,0:T(8,128)(2,1)S(1)} %collective-permute-done.halo_ref, bf16[2,4,64,1024]{3,2,1,0:T(8,128)(2,1)S(1)} %get-tuple-element.14.first_ref.now_ref, bf16[4,2,16,128]{3,2,1,0:T(8,128)(2,1)S(1)} %collective-permute-done.2.back_ref, ...), custom_call_target="tpu_custom_call" | custom-call | flops 301989888 | bytes 3145728 | tf_op jit(solution)/shard_map/first_time/pallas_call | solution.py:351
  19.5 20.0 %all_to_all.5.got_ref = bf16[32,64,128]{2,1,0:T(8,128)(2,1)S(1)} all-to-all(bf16[32,64,128]{2,1,0:T(8,128)(2,1)S(1)} %first_time.1), channel_id=1, replica_groups=mesh['freq'=32,'tm'=4] {'freq'}, dimensions={0} | all-to-all | bytes 1048576 | tf_op jit(solution)/shard_map/all_to_all | solution.py:361
  39.5 1.1 %join_channels.1 = f32[16,2,4,2048]{3,2,1,0:T(4,128)} custom-call(bf16[32,64,128]{2,1,0:T(8,128)(2,1)S(1)} %all_to_all.5.got_ref), custom_call_target="tpu_custom_call" | custom-call | tf_op jit(solution)/shard_map/join_channels/pallas_call | solution.py:364
Async XLA Ops:
  0.0 7.9 %copy-start.1 = (bf16[2,256,256]{2,1,0:T(8,128)(2,1)S(1)}, bf16[2,256,256]{2,1,0:T(8,128)(2,1)}, u32[]{:S(2)}) copy-start(bf16[2,256,256]{2,1,0:T(8,128)(2,1)} %constant.2.clone.table_ref) | copy-start | bytes 786436
  0.0 5.9 %copy-start = (bf16[2,256,4,1024]{3,2,1,0:T(4,128)(2,1)S(1)}, bf16[2,256,4,1024]{3,2,1,0:T(4,128)(2,1)}, u32[]{:S(2)}) copy-start(bf16[2,256,4,1024]{3,2,1,0:T(4,128)(2,1)} %volt_ref.5) | copy-start | bytes 12582916
  0.0 7.8 %copy-start.3 = (f32[64]{0:T(128)S(1)}, f32[64]{0:T(128)}, u32[]{:S(2)}) copy-start(f32[64]{0:T(128)} %param.6) | copy-start | bytes 772
  0.0 7.8 %copy-start.2 = (f32[2,4,1024]{2,1,0:T(4,128)S(1)}, f32[2,4,1024]{2,1,0:T(4,128)}, u32[]{:S(2)}) copy-start(f32[2,4,1024]{2,1,0:T(4,128)} %gains_ref.7) | copy-start | bytes 98308
  1.4 17.2 %collective-permute-start = (bf16[2,3,48,1024]{3,2,1,0:T(8,128)(2,1)S(1)}, bf16[2,3,48,1024]{3,2,1,0:T(8,128)(2,1)S(1)}, u32[]{:S(2)}, u32[]{:S(2)}) collective-permute-start(bf16[2,3,48,1024]{3,2,1,0:T(8,128)(2,1)S(1)} %block_tail.1), channel_id=1, source_target_pairs={{0,1},{1,2},{2,3},{4,5},{5,6},{6,7},{8,9},{9,10},{10,11},{12,13},{... | collective-permute-start | bytes 1769480 | tf_op jit(solution)/shard_map/ppermute | solution.py:292
  6.3 7.1 %collective-permute-start.1 = (bf16[2,48,1024]{2,1,0:T(8,128)(2,1)S(1)}, bf16[2,48,1024]{2,1,0:T(8,128)(2,1)S(1)}, u32[]{:S(2)}, u32[]{:S(2)}) collective-permute-start(bf16[2,48,1024]{2,1,0:T(8,128)(2,1)S(1)} %get-tuple-element.15), channel_id=1, source_target_pairs={{1,0},{2,1},{3,2},{0,3},{5,4},{6,5},{7,6},{4,7},{9,8},{10,9},{11,1... | collective-permute-start | bytes 589832 | tf_op jit(solution)/shard_map/ppermute | solution.py:305
  13.9 4.7 %collective-permute-start.2 = (bf16[4,2,16,128]{3,2,1,0:T(8,128)(2,1)S(1)}, bf16[4,2,16,128]{3,2,1,0:T(8,128)(2,1)S(1)}, u32[]{:S(2)}, u32[]{:S(2)}) collective-permute-start(bf16[4,2,16,128]{3,2,1,0:T(8,128)(2,1)S(1)} %next_block.1), channel_id=1, source_target_pairs={{0,1},{1,2},{2,3},{3,0},{4,5},{5,6},{6,7},{7,4},{8,9},{9,10},{10,1... | collective-permute-start | bytes 98312 | tf_op jit(solution)/shard_map/ppermute | solution.py:350

commit v3 on v2

--- a/solution.py
+++ b/solution.py
@@ -78,11 +78,13 @@
     return (rs + rv, it + iv), (rd + iw, iu - rw), (rs - rv, it - iv), (rd - iw, iu + rw)
 
 
-def powers(bank, data_of, channels, frames, gains_ref, table_ref, left_ref):
+def powers(bank, data_of, channels, frames, gains_ref, table_ref, left_ref, known_ref=None):
     count = len(channels)
     rows = frames * count * FINE
     for at, c in enumerate(channels):
         spec = jnp.dot(bank, data_of(c), preferred_element_type=F32)
+        if known_ref is not None:
+            spec = spec + known_ref[c]
         beams = steer(spec, gains_ref[0, c : c + 1], gains_ref[1, c : c + 1])
         for g in range(EW):
             for part in range(2):
@@ -121,6 +123,11 @@
     return jnp.concatenate([bank_ref[: FINE * EARLY], bank_ref[64 : 64 + FINE * EARLY]], axis=0)
 
 
+def half_bank(bank_ref, now):
+    bank, at = early_bank(bank_ref), SPAN * now
+    return jnp.concatenate([bank[:, at : at + SPAN], bank[:, 128 + at : 128 + at + SPAN]], axis=1)
+
+
 def tail_kernel(volt_ref, ahead_ref, tail_ref, sems):
     start = volt_ref.shape[1] - PAST
     copies = [
@@ -162,7 +169,7 @@
 
 def second_kernel(
     volt_ref, first_ref, gains_ref, table_ref, window_ref,
-    out_ref, bank_ref, late_ref, second_ref, ahead_ref, block_ref, left_ref, sems,
+    out_ref, bank_ref, known_ref, late_ref, second_ref, ahead_ref, block_ref, left_ref, sems,
 ):
     to = [block_ref] + [ahead_ref.at[i] for i in range(TIMES - 2)]
     copies = [
@@ -172,6 +179,9 @@
     for copy in copies:
         copy.start()
     fill_bank(window_ref, bank_ref)
+    for c in range(AHEAD):
+        own = jnp.concatenate([first_ref[0, c], first_ref[1, c]], axis=0)
+        known_ref[c] = jnp.dot(half_bank(bank_ref, 1), own, preferred_element_type=F32)
     sums = powers(
         jnp.concatenate([bank_ref[48:64], bank_ref[112:128]], axis=0),
         lambda c: jnp.concatenate([first_ref[0, c], first_ref[0, c], first_ref[1, c], first_ref[1, c]], axis=0),
@@ -215,18 +225,18 @@
 
 
 def first_kernel(
-    halo_ref, now_ref, back_ref, late_ref, gains_ref, table_ref, bank_ref, second_ref, later_ref,
+    halo_ref, known_ref, back_ref, late_ref, gains_ref, table_ref, bank_ref, second_ref, later_ref,
     out_ref, left_ref,
 ):
     out_ref[:, HALF : 2 * HALF] = second_ref[...]
     out_ref[:, 2 * HALF :] = later_ref[...]
     pad = jnp.zeros((SPAN - PAST, FEEDS), BF16)
     sums = powers(
-        early_bank(bank_ref),
+        half_bank(bank_ref, 0),
         lambda c: jnp.concatenate(
-            [pad, halo_ref[0, c], now_ref[0, c], pad, halo_ref[1, c], now_ref[1, c]], axis=0
+            [pad, halo_ref[0, c], pad, halo_ref[1, c]], axis=0
         ),
-        range(AHEAD), EARLY, gains_ref, table_ref, left_ref,
+        range(AHEAD), EARLY, gains_ref, table_ref, left_ref, known_ref,
     )
     for g in range(EW):
         power = [
@@ -307,13 +317,14 @@
     def powers_of(times):
         return jax.ShapeDtypeStruct((GROUP, times * HALF, 128), BF16)
 
-    power_1, bank, late, second, blocks = pl.pallas_call(
+    power_1, bank, known, late, second, blocks = pl.pallas_call(
         second_kernel,
         in_specs=[HBM] + [VMEM] * 4,
-        out_specs=[VMEM] * 5,
+        out_specs=[VMEM] * 6,
         out_shape=[
             powers_of(1),
             jax.ShapeDtypeStruct((128, 256), BF16),
+            jax.ShapeDtypeStruct((AHEAD, 2 * EARLY * FINE, FEEDS), F32),
             jax.ShapeDtypeStruct((EW, 2, SPAN, NS // 2), F32),
             jax.ShapeDtypeStruct((2, CHAN, SPAN, FEEDS), BF16),
             jax.ShapeDtypeStruct((TIMES - 2, 2, SPAN, CHAN, FEEDS), BF16),
@@ -357,7 +368,7 @@
         compiler_params=params(24),
         cost_estimate=cost(576, 3 << 20),
         name="first_time",
-    )(halo, first, returned, late, gains, table, bank, power_1, power_23)
+    )(halo, known, returned, late, gains, table, bank, power_1, power_23)
     got = lax.all_to_all(power, "freq", split_axis=0, concat_axis=0, tiled=True)
     chunks = 8
     wide = GROUP * CHAN * FINE

time: 40.8 us -> 41 us (level)
  no operation moved by 1% of the time
where the time goes in v3:
time: 41 us; the launch traced here: 40.8 us
  blocking collectives  20.1 us (49%)
  Pallas kernels  10 us (24%)
  starting transfers between devices  6.32 us (15%)
  waiting for transfers between devices  4.24 us (10%)
    all_to_all x1, blocking collectives, body(): got = lax.all_to_all(power, 'freq', split_axis=0, concat_axis=0, tiled=True)  20.1 us
    ppermute x1, starting transfers between devices, body(): halo = lax.ppermute(ahead, 'tm', forward[:-1])  4.54 us
    ppermute x1, waiting for transfers between devices, body(): returned = lax.ppermute(returned, 'tm', forward)  4.23 us
    pallas_call x1, Pallas kernels, body(): pl.pallas_call(later_kernel, in_specs=[VMEM] * 5, out_specs=[VMEM] * 2, o...  2.95 us
    pallas_call x1, Pallas kernels, body(): pl.pallas_call(second_kernel, in_specs=[HBM] + [VMEM] * 4, out_specs=[VME...  2.82 us
    ppermute x1, starting transfers between devices, body(): head = lax.ppermute(back, 'tm', backward)  1.54 us
    pallas_call x1, Pallas kernels, body(): pl.pallas_call(tail_kernel, in_specs=[HBM], out_specs=VMEM, out_shape=jax...  1.36 us
    pallas_call x1, Pallas kernels, body(): pl.pallas_call(join_kernel, in_specs=[VMEM], out_specs=HBM, out_shape=jax...  1.14 us
  transfers between devices with their start and end apart: 3, of which 1 were waited for; matrix products, arithmetic and copies ran while one was open for 0% of the time, Pallas kernels for 16%

profile of v3, /device:TPU:1, one launch (start us, length us, event | category | flops | bytes accessed | tf_op | source)
XLA Modules:
  0.0 40.8 jit_solution(7723579287935327007)
XLA Ops:
  0.0 0.0 copy-start
  0.0 1.4 %block_tail.1 = bf16[2,3,48,1024]{3,2,1,0:T(8,128)(2,1)S(1)} custom-call(bf16[2,256,4,1024]{3,2,1,0:T(4,128)(2,1)} %volt_ref.5), custom_call_target="tpu_custom_call" | custom-call | tf_op jit(solution)/shard_map/block_tail/pallas_call | solution.py:291
  1.4 0.0 copy-start.1
  1.4 0.0 copy-start.2
  1.4 0.0 copy-start.3
  1.4 4.5 %collective-permute-start = (bf16[2,3,48,1024]{3,2,1,0:T(8,128)(2,1)S(1)}, bf16[2,3,48,1024]{3,2,1,0:T(8,128)(2,1)S(1)}, u32[]{:S(2)}, u32[]{:S(2)}) collective-permute-start(bf16[2,3,48,1024]{3,2,1,0:T(8,128)(2,1)S(1)} %block_tail.1), channel_id=1, source_target_pairs={{0,1},{1,2},{2,3},{4,5},{5,6},{6,7},{8,9},{9,10},{10,11},{12,13},{... | collective-permute-start | bytes 1769480 | tf_op jit(solution)/shard_map/ppermute | solution.py:302
  6.0 0.0 copy-done
  6.0 0.4 block_head.1
  6.3 1.5 %collective-permute-start.1 = (bf16[2,48,1024]{2,1,0:T(8,128)(2,1)S(1)}, bf16[2,48,1024]{2,1,0:T(8,128)(2,1)S(1)}, u32[]{:S(2)}, u32[]{:S(2)}) collective-permute-start(bf16[2,48,1024]{2,1,0:T(8,128)(2,1)S(1)} %get-tuple-element.17), channel_id=1, source_target_pairs={{1,0},{2,1},{3,2},{0,3},{5,4},{6,5},{7,6},{4,7},{9,8},{10,9},{11,1... | collective-permute-start | bytes 589832 | tf_op jit(solution)/shard_map/ppermute | solution.py:315
  7.9 0.0 copy-done.1
  7.9 0.0 copy-done.2
  7.9 0.0 copy-done.3
  7.9 2.8 %second_time.1 = (bf16[32,16,128]{2,1,0:T(8,128)(2,1)S(1)}, bf16[128,256]{1,0:T(8,128)(2,1)S(1)}, f32[3,96,1024]{2,1,0:T(8,128)S(1)}, f32[4,2,64,128]{3,2,1,0:T(...) custom-call(bf16[2,256,4,1024]{3,2,1,0:T(4,128)(2,1)S(1)} %copy-done, ...), custom_call_target="tpu_custom_call" | custom-call | flops 671088640 | bytes 4194304 | tf_op jit(solution)/shard_map/second_time/pallas_call | solution.py:320
  10.7 3.0 %later_times.1 = (bf16[32,32,128]{2,1,0:T(8,128)(2,1)S(1)}, bf16[2,48,1024]{2,1,0:T(8,128)(2,1)S(1)}) custom-call(bf16[2,2,64,4,1024]{4,3,2,1,0:T(4,128)(2,1)S(1)} %get-tuple-element.18.ahead_ref, bf16[2,4,64,1024]{3,2,1,0:T(8,128)(2,1)S(1)} %get-tuple-element.19.second_ref, f32[2,4,1024]{2,1,0:T(4,128)S(1)} %copy-done.2, ...), custom_call_target="tpu_custom_call" | custom-call | flops 1073741824 | bytes 4194304 | tf_op jit(solution)/shard_map/later_times/pallas_call | solution.py:341
  13.7 0.0 collective-permute-done.1.head_ref
  13.7 0.4 %next_block.1 = bf16[4,2,16,128]{3,2,1,0:T(8,128)(2,1)S(1)} custom-call(bf16[2,48,1024]{2,1,0:T(8,128)(2,1)S(1)} %collective-permute-done.1.head_ref, bf16[2,48,1024]{2,1,0:T(8,128)(2,1)S(1)} %get-tuple-element.21.keep_ref, f32[2,4,1024]{2,1,0:T(4,128)S(1)} %copy-done.2, bf16[2,256,256]{2,1,0:T(8,128)(2,1)S(1)} %copy-done.1, ...), custom_call_target="tpu_custom_call" | custom-call | flops 100663296 | bytes 1048576 | tf_op jit(solution)/shard_map/next_block/pallas_call | solution.py:351
  14.1 0.2 collective-permute-start.2
  14.4 4.2 %collective-permute-done.2.back_ref = bf16[4,2,16,128]{3,2,1,0:T(8,128)(2,1)S(1)} collective-permute-done((bf16[4,2,16,128]{3,2,1,0:T(8,128)(2,1)S(1)}, bf16[4,2,16,128]{3,2,1,0:T(8,128)(2,1)S(1)}, u32[]{:S(2)}, u32[]{:S(2)}) %collective-permute-start.2) | collective-permute-done | bytes 32800 | tf_op jit(solution)/shard_map/ppermute | solution.py:361
  18.6 0.0 collective-permute-done.halo_ref
  18.6 1.0 %first_time.1 = bf16[32,64,128]{2,1,0:T(8,128)(2,1)S(1)} custom-call(bf16[2,3,48,1024]{3,2,1,0:T(8,128)(2,1)S(1)} %collective-permute-done.halo_ref, f32[3,96,1024]{2,1,0:T(8,128)S(1)} %get-tuple-element.16.known_ref, bf16[4,2,16,128]{3,2,1,0:T(8,128)(2,1)S(1)} %collective-permute-done.2.back_ref, f32[4,2,64,128]{3,2,1,0:T(8,128)S(1)} %get-tuple-element.22.late_ref, ...), custom_call_target="tpu_custom_call" | custom-call | flops 301989888 | bytes 3145728 | tf_op jit(solution)/shard_map/first_time/pallas_call | solution.py:362
  19.6 20.1 %all_to_all.5.got_ref = bf16[32,64,128]{2,1,0:T(8,128)(2,1)S(1)} all-to-all(bf16[32,64,128]{2,1,0:T(8,128)(2,1)S(1)} %first_time.1), channel_id=1, replica_groups=mesh['freq'=32,'tm'=4] {'freq'}, dimensions={0} | all-to-all | bytes 1048576 | tf_op jit(solution)/shard_map/all_to_all | solution.py:372
  39.7 1.1 %join_channels.1 = f32[16,2,4,2048]{3,2,1,0:T(4,128)} custom-call(bf16[32,64,128]{2,1,0:T(8,128)(2,1)S(1)} %all_to_all.5.got_ref), custom_call_target="tpu_custom_call" | custom-call | tf_op jit(solution)/shard_map/join_channels/pallas_call | solution.py:375
Async XLA Ops:
  0.0 6.0 %copy-start = (bf16[2,256,4,1024]{3,2,1,0:T(4,128)(2,1)S(1)}, bf16[2,256,4,1024]{3,2,1,0:T(4,128)(2,1)}, u32[]{:S(2)}) copy-start(bf16[2,256,4,1024]{3,2,1,0:T(4,128)(2,1)} %volt_ref.5) | copy-start | bytes 12582916
  1.4 6.5 %copy-start.1 = (bf16[2,256,256]{2,1,0:T(8,128)(2,1)S(1)}, bf16[2,256,256]{2,1,0:T(8,128)(2,1)}, u32[]{:S(2)}) copy-start(bf16[2,256,256]{2,1,0:T(8,128)(2,1)} %constant.2.clone.table_ref) | copy-start | bytes 786436
  1.4 6.5 %copy-start.2 = (f32[2,4,1024]{2,1,0:T(4,128)S(1)}, f32[2,4,1024]{2,1,0:T(4,128)}, u32[]{:S(2)}) copy-start(f32[2,4,1024]{2,1,0:T(4,128)} %gains_ref.7) | copy-start | bytes 98308
  1.4 6.5 %copy-start.3 = (f32[64]{0:T(128)S(1)}, f32[64]{0:T(128)}, u32[]{:S(2)}) copy-start(f32[64]{0:T(128)} %param.6) | copy-start | bytes 772
  1.4 17.2 %collective-permute-start = (bf16[2,3,48,1024]{3,2,1,0:T(8,128)(2,1)S(1)}, bf16[2,3,48,1024]{3,2,1,0:T(8,128)(2,1)S(1)}, u32[]{:S(2)}, u32[]{:S(2)}) collective-permute-start(bf16[2,3,48,1024]{3,2,1,0:T(8,128)(2,1)S(1)} %block_tail.1), channel_id=1, source_target_pairs={{0,1},{1,2},{2,3},{4,5},{5,6},{6,7},{8,9},{9,10},{10,11},{12,13},{... | collective-permute-start | bytes 1769480 | tf_op jit(solution)/shard_map/ppermute | solution.py:302
  6.3 7.3 %collective-permute-start.1 = (bf16[2,48,1024]{2,1,0:T(8,128)(2,1)S(1)}, bf16[2,48,1024]{2,1,0:T(8,128)(2,1)S(1)}, u32[]{:S(2)}, u32[]{:S(2)}) collective-permute-start(bf16[2,48,1024]{2,1,0:T(8,128)(2,1)S(1)} %get-tuple-element.17), channel_id=1, source_target_pairs={{1,0},{2,1},{3,2},{0,3},{5,4},{6,5},{7,6},{4,7},{9,8},{10,9},{11,1... | collective-permute-start | bytes 589832 | tf_op jit(solution)/shard_map/ppermute | solution.py:315
  14.1 4.5 %collective-permute-start.2 = (bf16[4,2,16,128]{3,2,1,0:T(8,128)(2,1)S(1)}, bf16[4,2,16,128]{3,2,1,0:T(8,128)(2,1)S(1)}, u32[]{:S(2)}, u32[]{:S(2)}) collective-permute-start(bf16[4,2,16,128]{3,2,1,0:T(8,128)(2,1)S(1)} %next_block.1), channel_id=1, source_target_pairs={{0,1},{1,2},{2,3},{3,0},{4,5},{5,6},{6,7},{7,4},{8,9},{9,10},{10,1... | collective-permute-start | bytes 98312 | tf_op jit(solution)/shard_map/ppermute | solution.py:361

commit v4 on v2

--- a/solution.py
+++ b/solution.py
@@ -218,8 +218,6 @@
     halo_ref, now_ref, back_ref, late_ref, gains_ref, table_ref, bank_ref, second_ref, later_ref,
     out_ref, left_ref,
 ):
-    out_ref[:, HALF : 2 * HALF] = second_ref[...]
-    out_ref[:, 2 * HALF :] = later_ref[...]
     pad = jnp.zeros((SPAN - PAST, FEEDS), BF16)
     sums = powers(
         early_bank(bank_ref),
@@ -234,6 +232,8 @@
             for odd in range(2)
         ]
         out_ref[8 * g : 8 * (g + 1), :HALF] = by_beam(*power)
+    out_ref[:, HALF : 2 * HALF] = second_ref[...]
+    out_ref[:, 2 * HALF :] = later_ref[...]
 
 
 def join_kernel(got_ref, out_ref, joined_ref, sems):

time: 40.8 us -> 40.8 us (level)
  no operation moved by 1% of the time
where the time goes in v4:
time: 40.8 us; the launch traced here: 40.6 us
  blocking collectives  20 us (49%)
  Pallas kernels  9.76 us (24%)
  starting transfers between devices  6.32 us (15%)
  waiting for transfers between devices  4.48 us (11%)
    all_to_all x1, blocking collectives, body(): got = lax.all_to_all(power, 'freq', split_axis=0, concat_axis=0, tiled=True)  20 us
    ppermute x1, starting transfers between devices, body(): halo = lax.ppermute(ahead, 'tm', forward[:-1])  4.54 us
    ppermute x1, waiting for transfers between devices, body(): returned = lax.ppermute(returned, 'tm', forward)  4.47 us
    pallas_call x1, Pallas kernels, body(): pl.pallas_call(later_kernel, in_specs=[VMEM] * 5, out_specs=[VMEM] * 2, o...  2.95 us
    pallas_call x1, Pallas kernels, body(): pl.pallas_call(second_kernel, in_specs=[HBM] + [VMEM] * 4, out_specs=[VME...  2.59 us
    ppermute x1, starting transfers between devices, body(): head = lax.ppermute(back, 'tm', backward)  1.54 us
    pallas_call x1, Pallas kernels, body(): pl.pallas_call(tail_kernel, in_specs=[HBM], out_specs=VMEM, out_shape=jax...  1.36 us
    pallas_call x1, Pallas kernels, body(): pl.pallas_call(join_kernel, in_specs=[VMEM], out_specs=HBM, out_shape=jax...  1.14 us
  transfers between devices with their start and end apart: 3, of which 1 were waited for; matrix products, arithmetic and copies ran while one was open for 0% of the time, Pallas kernels for 16%

profile of v4, /device:TPU:1, one launch (start us, length us, event | category | flops | bytes accessed | tf_op | source)
XLA Modules:
  0.0 40.6 jit_solution(14531188108159918551)
XLA Ops:
  0.0 0.0 copy-start.1
  0.0 0.0 copy-start
  0.0 0.0 copy-start.3
  0.0 0.0 copy-start.2
  0.0 1.4 %block_tail.1 = bf16[2,3,48,1024]{3,2,1,0:T(8,128)(2,1)S(1)} custom-call(bf16[2,256,4,1024]{3,2,1,0:T(4,128)(2,1)} %volt_ref.5), custom_call_target="tpu_custom_call" | custom-call | tf_op jit(solution)/shard_map/block_tail/pallas_call | solution.py:281
  1.4 4.5 %collective-permute-start = (bf16[2,3,48,1024]{3,2,1,0:T(8,128)(2,1)S(1)}, bf16[2,3,48,1024]{3,2,1,0:T(8,128)(2,1)S(1)}, u32[]{:S(2)}, u32[]{:S(2)}) collective-permute-start(bf16[2,3,48,1024]{3,2,1,0:T(8,128)(2,1)S(1)} %block_tail.1), channel_id=1, source_target_pairs={{0,1},{1,2},{2,3},{4,5},{5,6},{6,7},{8,9},{9,10},{10,11},{12,13},{... | collective-permute-start | bytes 1769480 | tf_op jit(solution)/shard_map/ppermute | solution.py:292
  5.9 0.0 copy-done
  5.9 0.4 block_head.1
  6.3 1.5 %collective-permute-start.1 = (bf16[2,48,1024]{2,1,0:T(8,128)(2,1)S(1)}, bf16[2,48,1024]{2,1,0:T(8,128)(2,1)S(1)}, u32[]{:S(2)}, u32[]{:S(2)}) collective-permute-start(bf16[2,48,1024]{2,1,0:T(8,128)(2,1)S(1)} %get-tuple-element.15), channel_id=1, source_target_pairs={{1,0},{2,1},{3,2},{0,3},{5,4},{6,5},{7,6},{4,7},{9,8},{10,9},{11,1... | collective-permute-start | bytes 589832 | tf_op jit(solution)/shard_map/ppermute | solution.py:305
  7.8 0.0 copy-done.1
  7.9 0.0 copy-done.3
  7.9 0.0 copy-done.2
  7.9 2.6 %second_time.1 = (bf16[32,16,128]{2,1,0:T(8,128)(2,1)S(1)}, bf16[128,256]{1,0:T(8,128)(2,1)S(1)}, f32[4,2,64,128]{3,2,1,0:T(8,128)S(1)}, bf16[2,4,64,1024]{3,2,1...) custom-call(bf16[2,256,4,1024]{3,2,1,0:T(4,128)(2,1)S(1)} %copy-done, ...), custom_call_target="tpu_custom_call" | custom-call | flops 671088640 | bytes 4194304 | tf_op jit(solution)/shard_map/second_time/pallas_call | solution.py:310
  10.5 2.9 %later_times.1 = (bf16[32,32,128]{2,1,0:T(8,128)(2,1)S(1)}, bf16[2,48,1024]{2,1,0:T(8,128)(2,1)S(1)}) custom-call(bf16[2,2,64,4,1024]{4,3,2,1,0:T(4,128)(2,1)S(1)} %get-tuple-element.16.ahead_ref, bf16[2,4,64,1024]{3,2,1,0:T(8,128)(2,1)S(1)} %get-tuple-element.17.second_ref, f32[2,4,1024]{2,1,0:T(4,128)S(1)} %copy-done.2, ...), custom_call_target="tpu_custom_call" | custom-call | flops 1073741824 | bytes 4194304 | tf_op jit(solution)/shard_map/later_times/pallas_call | solution.py:330
  13.4 0.0 collective-permute-done.1.head_ref
  13.4 0.4 %next_block.1 = bf16[4,2,16,128]{3,2,1,0:T(8,128)(2,1)S(1)} custom-call(bf16[2,48,1024]{2,1,0:T(8,128)(2,1)S(1)} %collective-permute-done.1.head_ref, bf16[2,48,1024]{2,1,0:T(8,128)(2,1)S(1)} %get-tuple-element.19.keep_ref, f32[2,4,1024]{2,1,0:T(4,128)S(1)} %copy-done.2, bf16[2,256,256]{2,1,0:T(8,128)(2,1)S(1)} %copy-done.1, ...), custom_call_target="tpu_custom_call" | custom-call | flops 100663296 | bytes 1048576 | tf_op jit(solution)/shard_map/next_block/pallas_call | solution.py:340
  13.9 0.2 collective-permute-start.2
  14.1 4.5 %collective-permute-done.2.back_ref = bf16[4,2,16,128]{3,2,1,0:T(8,128)(2,1)S(1)} collective-permute-done((bf16[4,2,16,128]{3,2,1,0:T(8,128)(2,1)S(1)}, bf16[4,2,16,128]{3,2,1,0:T(8,128)(2,1)S(1)}, u32[]{:S(2)}, u32[]{:S(2)}) %collective-permute-start.2) | collective-permute-done | bytes 32800 | tf_op jit(solution)/shard_map/ppermute | solution.py:350
  18.6 0.0 collective-permute-done.halo_ref
  18.6 0.9 %first_time.1 = bf16[32,64,128]{2,1,0:T(8,128)(2,1)S(1)} custom-call(bf16[2,3,48,1024]{3,2,1,0:T(8,128)(2,1)S(1)} %collective-permute-done.halo_ref, bf16[2,4,64,1024]{3,2,1,0:T(8,128)(2,1)S(1)} %get-tuple-element.14.first_ref.now_ref, bf16[4,2,16,128]{3,2,1,0:T(8,128)(2,1)S(1)} %collective-permute-done.2.back_ref, ...), custom_call_target="tpu_custom_call" | custom-call | flops 301989888 | bytes 3145728 | tf_op jit(solution)/shard_map/first_time/pallas_call | solution.py:351
  19.5 20.0 %all_to_all.5.got_ref = bf16[32,64,128]{2,1,0:T(8,128)(2,1)S(1)} all-to-all(bf16[32,64,128]{2,1,0:T(8,128)(2,1)S(1)} %first_time.1), channel_id=1, replica_groups=mesh['freq'=32,'tm'=4] {'freq'}, dimensions={0} | all-to-all | bytes 1048576 | tf_op jit(solution)/shard_map/all_to_all | solution.py:361
  39.5 1.1 %join_channels.1 = f32[16,2,4,2048]{3,2,1,0:T(4,128)} custom-call(bf16[32,64,128]{2,1,0:T(8,128)(2,1)S(1)} %all_to_all.5.got_ref), custom_call_target="tpu_custom_call" | custom-call | tf_op jit(solution)/shard_map/join_channels/pallas_call | solution.py:364
Async XLA Ops:
  0.0 7.9 %copy-start.1 = (bf16[2,256,256]{2,1,0:T(8,128)(2,1)S(1)}, bf16[2,256,256]{2,1,0:T(8,128)(2,1)}, u32[]{:S(2)}) copy-start(bf16[2,256,256]{2,1,0:T(8,128)(2,1)} %constant.2.clone.table_ref) | copy-start | bytes 786436
  0.0 5.9 %copy-start = (bf16[2,256,4,1024]{3,2,1,0:T(4,128)(2,1)S(1)}, bf16[2,256,4,1024]{3,2,1,0:T(4,128)(2,1)}, u32[]{:S(2)}) copy-start(bf16[2,256,4,1024]{3,2,1,0:T(4,128)(2,1)} %volt_ref.5) | copy-start | bytes 12582916
  0.0 7.8 %copy-start.3 = (f32[64]{0:T(128)S(1)}, f32[64]{0:T(128)}, u32[]{:S(2)}) copy-start(f32[64]{0:T(128)} %param.6) | copy-start | bytes 772
  0.0 7.8 %copy-start.2 = (f32[2,4,1024]{2,1,0:T(4,128)S(1)}, f32[2,4,1024]{2,1,0:T(4,128)}, u32[]{:S(2)}) copy-start(f32[2,4,1024]{2,1,0:T(4,128)} %gains_ref.7) | copy-start | bytes 98308
  1.4 17.2 %collective-permute-start = (bf16[2,3,48,1024]{3,2,1,0:T(8,128)(2,1)S(1)}, bf16[2,3,48,1024]{3,2,1,0:T(8,128)(2,1)S(1)}, u32[]{:S(2)}, u32[]{:S(2)}) collective-permute-start(bf16[2,3,48,1024]{3,2,1,0:T(8,128)(2,1)S(1)} %block_tail.1), channel_id=1, source_target_pairs={{0,1},{1,2},{2,3},{4,5},{5,6},{6,7},{8,9},{9,10},{10,11},{12,13},{... | collective-permute-start | bytes 1769480 | tf_op jit(solution)/shard_map/ppermute | solution.py:292
  6.3 7.1 %collective-permute-start.1 = (bf16[2,48,1024]{2,1,0:T(8,128)(2,1)S(1)}, bf16[2,48,1024]{2,1,0:T(8,128)(2,1)S(1)}, u32[]{:S(2)}, u32[]{:S(2)}) collective-permute-start(bf16[2,48,1024]{2,1,0:T(8,128)(2,1)S(1)} %get-tuple-element.15), channel_id=1, source_target_pairs={{1,0},{2,1},{3,2},{0,3},{5,4},{6,5},{7,6},{4,7},{9,8},{10,9},{11,1... | collective-permute-start | bytes 589832 | tf_op jit(solution)/shard_map/ppermute | solution.py:305
  13.9 4.7 %collective-permute-start.2 = (bf16[4,2,16,128]{3,2,1,0:T(8,128)(2,1)S(1)}, bf16[4,2,16,128]{3,2,1,0:T(8,128)(2,1)S(1)}, u32[]{:S(2)}, u32[]{:S(2)}) collective-permute-start(bf16[4,2,16,128]{3,2,1,0:T(8,128)(2,1)S(1)} %next_block.1), channel_id=1, source_target_pairs={{0,1},{1,2},{2,3},{3,0},{4,5},{5,6},{6,7},{7,4},{8,9},{9,10},{10,1... | collective-permute-start | bytes 98312 | tf_op jit(solution)/shard_map/ppermute | solution.py:350
